TPU v7x, 256 devices: a whole 4x4x8 slice. The times are simulated.
256 devices in a mesh: dp: 32 (over x_hi, z, core), tensor: 8 (over x_lo, y).
Axes of the slice: x: 4 (x_hi: 2, x_lo: 2; x = x_hi * 2 + x_lo), y: 4, z: 8, core: 2. Of those that a mesh axis runs over, the one named last changes fastest.
Arguments:
- prompt_x: bfloat16 [4096, 5120], P('dp'), may hold values from -6 to 6
- key_matrix: bfloat16 [5120, 1024], P(None, 'tensor'), may hold values from -0.078125 to 0.078125
- value_matrix: bfloat16 [5120, 1024], P(None, 'tensor'), may hold values from -0.078125 to 0.078125
- k_gain: float32 [128], replicated, may hold values from 0.1 to 1.9
- queries: bfloat16 [8192, 8192], P('dp', 'tensor'), may hold values from -64 to 64
- response_keys: bfloat16 [8192, 1024], P('dp', 'tensor'), may hold values from -6 to 6
- response_values: bfloat16 [8192, 1024], P('dp', 'tensor'), may hold values from -6 to 6
- output_gradient: bfloat16 [8192, 8192], P('dp', 'tensor'), may hold values from -96 to 96
- response_counts: int32 [32], replicated, may hold values from 1 to 2, as said below
- slot_prompt: int32 [64], replicated, may hold values from 0 to 15
- prompt_owner: int32 [16], replicated, may hold values from 0 to 15, each once
- prompt_lengths: int32 [16], replicated, may hold values from 64 to 256, as said below
Outputs:
- d_queries: bfloat16 [8192, 8192], P('dp', 'tensor')
- d_resp_keys: bfloat16 [8192, 1024], P('dp', 'tensor')
- d_resp_values: bfloat16 [8192, 1024], P('dp', 'tensor')
- d_prompt_x: bfloat16 [4096, 5120], P('dp', 'tensor')
Inputs may be any that keep to these rules, and one draw needn't show every extreme that they name: `response_counts`: some index of dp holds 2 responses. `slot_prompt`: slots at or beyond the count of their index of dp are unused. `prompt_owner`: a permutation; prompt p lies on dp indices prompt_owner[p] * 2 to prompt_owner[p] * 2 + 1, in order. `prompt_lengths`: some prompt has 256 tokens.
All inputs are finite; a program needn't handle non-finite values.
Results may differ from a plain program's by a relative error of at most 0.024.
Values may be sent and summed in bfloat16 or wider, within the bound.
No kernel may reach another device: no remote copies, remote signals or barrier semaphores. Data moves between devices by JAX's collectives and lax.ppermute only.
A program may use at most 64 MiB of HBM per device.

v0:
```python
import functools

import jax
import jax.numpy as jnp
import numpy as np
from jax import lax
from jax.experimental import pallas as pl
from jax.experimental.pallas import tpu as pltpu
from jax.sharding import Mesh
from jax.sharding import PartitionSpec as P

HEAD = 128
R_CAP = 2
RLEN = 128
PLEN = 256
HALF = 128
CHIPS = 16
CORES = 2
PIECE = HALF // CHIPS
UNIT = 2 * PIECE
WIDTH = 5120
TENSOR = 8
COLS = WIDTH // TENSOR
GROUPS = 8
SCALE = HEAD ** (-0.5)
EXP2_SCALE = SCALE * float(np.log2(np.e))
EPS = 1e-06
FAR = -1e30
PAIRS = 4
f32 = jnp.float32
bf16 = jnp.bfloat16
DP = ("x_hi", "z", "core")
SPREAD = ("x_hi", "z")
X_LO = 2
Y = 4
PROJECT_VMEM = 60 << 20
SMEM = pl.BlockSpec(memory_space=pltpu.SMEM)


def rope_table():
    freqs = 1000000.0 ** (-np.arange(HEAD // 2, dtype=np.float64) * 2.0 / HEAD)
    angles = np.arange(PLEN, dtype=np.float64)[:, None] * freqs[None, :]
    both = np.concatenate([np.cos(angles), np.sin(angles)], axis=1)
    return both.astype(np.float32).reshape(CORES, HALF, HEAD)


def cos_sin(table):
    first = lax.broadcasted_iota(jnp.int32, table.shape, 1) < HEAD // 2
    turned = swap_halves(table)
    return jnp.where(first, table, turned), jnp.where(first, -turned, table)


def swap_halves(u):
    return pltpu.roll(u, HEAD // 2, 1)


def to_units(keys, values):
    n = keys.shape[0] // PIECE
    return jnp.concatenate(
        [keys.reshape(n, PIECE, HEAD), values.reshape(n, PIECE, HEAD)], axis=1
    )


def from_units(units):
    u = units.astype(f32)
    n = u.shape[0]
    return u[:, :PIECE].reshape(n * PIECE, HEAD), u[:, PIECE:].reshape(n * PIECE, HEAD)


def dot_nn(a, b):
    return lax.dot_general(a, b, (((1,), (0,)), ((), ())), preferred_element_type=f32)


def dot_nt(a, b):
    return lax.dot_general(a, b, (((1,), (1,)), ((), ())), preferred_element_type=f32)


def project_kernel(
    x_ref, wk_ref, wv_ref, gain_ref, table_ref, units_ref, *refs
):
    send_refs, (x_s, w_s, table_s, sems, table_sem, send_sems) = refs[:Y - 1], refs[Y - 1:]
    core, y = lax.axis_index("core"), lax.axis_index("y")
    order = [(k, half) for k in range(1, Y) for half in range(X_LO)] + [(0, 0), (0, 1)]
    copies = []
    for n, (k, half) in enumerate(order):
        rows = pl.ds(pl.multiple_of((half * Y + (y ^ k)) * COLS, COLS), COLS)
        copies.append(
            [
                pltpu.make_async_copy(wk_ref.at[rows], w_s.at[n, 0], sems.at[n, 1]),
                pltpu.make_async_copy(wv_ref.at[rows], w_s.at[n, 1], sems.at[n, 2]),
                pltpu.make_async_copy(x_ref.at[:, rows], x_s.at[n], sems.at[n, 0]),
            ]
        )
        for copy in copies[-1]:
            copy.start()
    table = pltpu.make_async_copy(table_ref.at[core], table_s, table_sem)
    table.start()
    sends = [
        pltpu.make_async_copy(w_s.at[n], send_refs[k - 1].at[half], send_sems.at[n])
        for n, (k, half) in enumerate(order)
        if k
    ]
    acc = jnp.zeros((HALF, 2 * HEAD), f32)
    for n in range(TENSOR):
        for copy in copies[n]:
            copy.wait()
        if n < len(sends):
            sends[n].start()
        acc += dot_nn(x_s[n], jnp.concatenate([w_s[n, 0], w_s[n, 1]], axis=1))
    table.wait()
    cos, sin = cos_sin(table_s[...])
    raw = acc[:, :HEAD]
    inv = lax.rsqrt(jnp.mean(raw * raw, axis=-1, keepdims=True) + EPS)
    u = raw * inv * gain_ref[...]
    keys = u * cos + swap_halves(u) * sin
    high = raw.astype(bf16).astype(f32)
    parts = [keys, acc[:, HEAD:], high, raw - high]
    units_ref[...] = jnp.concatenate(
        [part.reshape(CHIPS, PIECE, HEAD) for part in parts], axis=1
    ).astype(bf16)
    for copy in sends:
        copy.wait()


def project(x, wk, wv, gain, table):
    vmem = pl.BlockSpec(memory_space=pltpu.VMEM)
    hbm = pl.BlockSpec(memory_space=pltpu.HBM)
    anywhere = pl.BlockSpec(memory_space=pl.ANY)
    return pl.pallas_call(
        project_kernel,
        in_specs=[hbm, hbm, hbm, vmem, hbm],
        out_specs=[vmem] + [anywhere] * (Y - 1),
        out_shape=[jax.ShapeDtypeStruct((CHIPS, 2 * UNIT, HEAD), bf16)]
        + [jax.ShapeDtypeStruct((X_LO, 2, COLS, HEAD), bf16)] * (Y - 1),
        scratch_shapes=[
            pltpu.VMEM((TENSOR, HALF, COLS), bf16),
            pltpu.VMEM((TENSOR, 2, COLS, HEAD), bf16),
            pltpu.VMEM((HALF, HEAD), f32),
            pltpu.SemaphoreType.DMA((TENSOR, 3)),
            pltpu.SemaphoreType.DMA(()),
            pltpu.SemaphoreType.DMA((TENSOR - X_LO,)),
        ],
        compiler_params=pltpu.CompilerParams(vmem_limit_bytes=PROJECT_VMEM),
        cost_estimate=pl.CostEstimate(flops=2 * HALF * WIDTH * 256, bytes_accessed=4 << 20, transcendentals=0),
        name="project",
    )(x, wk, wv, gain, table)


def select_kernel(slot_prompt_ref, owner_ref, mine_ref, other_ref, out_ref):
    core = lax.axis_index("core")
    for chip in range(CHIPS):
        for r in range(R_CAP):
            q = owner_ref[slot_prompt_ref[chip * CORES * R_CAP + core * R_CAP + r]]
            out_ref[chip, r, 0] = mine_ref[q, :UNIT]
            out_ref[chip, r, 1] = other_ref[q, :UNIT]


def select(slot_prompt, owner, mine, other):
    vmem = pl.BlockSpec(memory_space=pltpu.VMEM)
    return pl.pallas_call(
        select_kernel,
        in_specs=[SMEM, SMEM, vmem, vmem],
        out_specs=vmem,
        out_shape=jax.ShapeDtypeStruct((CHIPS, R_CAP, 2, UNIT, HEAD), bf16),
        compiler_params=pltpu.CompilerParams(vmem_limit_bytes=8 << 20),
        name="select",
    )(slot_prompt, owner, mine, other)


def attend_slot(core, length, live, kv_ref, q_ref, g_ref, rk_ref, rv_ref, dq_ref, drk_ref, drv_ref, grads_ref, ds_s, pb_s):
    ka, va = from_units(kv_ref[:, 0])
    kb, vb = from_units(kv_ref[:, 1])
    keys = jnp.concatenate([ka.astype(bf16), kb.astype(bf16), rk_ref[...]], axis=0)
    values = jnp.concatenate([va.astype(bf16), vb.astype(bf16), rv_ref[...]], axis=0)
    row = lax.broadcasted_iota(jnp.int32, (HALF, HEAD), 0)
    column = lax.broadcasted_iota(jnp.int32, (HALF, HEAD), 1)
    hidden = lambda first: jnp.where((column == 0) & (row + first >= length), FAR, 0.0)
    far = jnp.concatenate(
        [
            hidden(core * HALF),
            hidden((1 - core) * HALF),
            jnp.where((column == row) & (row > 0), FAR, 0.0),
        ],
        axis=0,
    ).astype(bf16)
    early = jnp.where((column == 0) | (column > row), 1.0, 0.0).astype(bf16)
    keys_far = jnp.concatenate([keys, far], axis=1)
    for h in range(0, GROUPS, PAIRS):
        cols = slice(h * HEAD, (h + PAIRS) * HEAD)
        stack = lambda ref: jnp.concatenate([ref[:, (h + i) * HEAD:(h + i + 1) * HEAD] for i in range(PAIRS)], axis=0)
        qh = jnp.concatenate([stack(q_ref), jnp.concatenate([early] * PAIRS, axis=0)], axis=1)
        st = dot_nt(keys_far, qh)
        dpt = dot_nt(values, stack(g_ref))
        top = jnp.max(st, axis=0, keepdims=True)
        e = jnp.exp2((st - top) * EXP2_SCALE)
        inv = 1.0 / jnp.sum(e, axis=0, keepdims=True)
        delta = jnp.sum(e * dpt, axis=0, keepdims=True) * inv
        p = e * inv
        pb_s[:, cols] = p.astype(bf16)
        ds_s[:, cols] = (p * (dpt - delta)).astype(bf16)
    rows_of = lambda ref: jnp.concatenate([ref[:, h * HEAD:(h + 1) * HEAD] for h in range(GROUPS)], axis=0)
    keep = jnp.where(live, 1.0, 0.0)
    kept = lambda x: x * keep
    dk = kept(dot_nn(ds_s[...], rows_of(q_ref)) * SCALE)
    dv = kept(dot_nn(pb_s[...], rows_of(g_ref)))
    grads_ref[:, 0] = to_units(dk[:HALF], dv[:HALF]).astype(bf16)
    grads_ref[:, 1] = to_units(dk[HALF:PLEN], dv[HALF:PLEN]).astype(bf16)
    drk_ref[...] = dk[PLEN:].astype(bf16)
    drv_ref[...] = dv[PLEN:].astype(bf16)
    keys_t = keys.T
    for h in range(GROUPS):
        cols = slice(h * HEAD, (h + 1) * HEAD)
        dq_ref[:, cols] = kept((dot_nn(keys_t, ds_s[:, cols]) * SCALE).T).astype(bf16)


def entry(ref, index):
    row = ref[...]
    here = lax.broadcasted_iota(jnp.int32, row.shape, 1) == index
    return jnp.sum(jnp.where(here, row, 0).astype(f32), axis=1, keepdims=True).astype(jnp.int32)


def attend_kernel(
    counts_ref, slot_prompt_ref, lengths_ref,
    kv_ref, q_ref, g_ref, rk_ref, rv_ref,
    dq_ref, drk_ref, drv_ref, grads_ref,
    ds_s, pb_s,
):
    core, dp = lax.axis_index("core"), lax.axis_index(DP)
    for slot in range(R_CAP):
        rows = pl.ds(slot * RLEN, RLEN)
        kv = kv_ref.at[:, slot]
        ins = [r.at[rows] for r in (q_ref, g_ref, rk_ref, rv_ref)]
        outs = [r.at[rows] for r in (dq_ref, drk_ref, drv_ref)] + [grads_ref.at[:, slot]]

        prompt = entry(slot_prompt_ref, dp * R_CAP + slot)
        length = entry(lengths_ref, prompt)
        live = entry(counts_ref, dp) > slot
        attend_slot(core, length, live, kv, *ins, *outs, ds_s.at[slot], pb_s.at[slot])


def attend(counts, slot_prompt, lengths, kv, q, g, rk, rv):
    width = GROUPS * HEAD
    vmem = pl.BlockSpec(memory_space=pltpu.VMEM)
    return pl.pallas_call(
        attend_kernel,
        in_specs=[vmem] * 8,
        out_specs=[vmem] * 4,
        out_shape=[
            jax.ShapeDtypeStruct((R_CAP * RLEN, width), bf16),
            jax.ShapeDtypeStruct((R_CAP * RLEN, HEAD), bf16),
            jax.ShapeDtypeStruct((R_CAP * RLEN, HEAD), bf16),
            jax.ShapeDtypeStruct((CHIPS, R_CAP, 2, UNIT, HEAD), bf16),
        ],
        scratch_shapes=[
            pltpu.VMEM((R_CAP, PLEN + RLEN, width), bf16),
            pltpu.VMEM((R_CAP, PLEN + RLEN, width), bf16),
        ],
        compiler_params=pltpu.CompilerParams(vmem_limit_bytes=16 << 20),
        cost_estimate=pl.CostEstimate(flops=10 * 2 * 384 * 1024 * 128, bytes_accessed=3 << 20, transcendentals=2 * 384 * 1024),
        name="attend",
    )(counts.reshape(1, -1), slot_prompt.reshape(1, -1), lengths.reshape(1, -1), kv, q, g, rk, rv)


def collect_kernel(slot_prompt_ref, owner_ref, got_ref, mine_ref, other_ref, acc):
    core = lax.axis_index("core")
    acc[...] = jnp.zeros_like(acc)
    for chip in range(CHIPS):
        for r in range(R_CAP):
            q = owner_ref[slot_prompt_ref[chip * CORES * R_CAP + core * R_CAP + r]]
            acc[q] += got_ref[chip, r].astype(f32)
    mine_ref[...] = acc[:, 0]
    other_ref[...] = acc[:, 1].astype(bf16)


def collect(slot_prompt, owner, got):
    vmem = pl.BlockSpec(memory_space=pltpu.VMEM)
    return pl.pallas_call(
        collect_kernel,
        in_specs=[SMEM, SMEM, vmem],
        out_specs=[vmem, vmem],
        out_shape=[
            jax.ShapeDtypeStruct((CHIPS, UNIT, HEAD), f32),
            jax.ShapeDtypeStruct((CHIPS, UNIT, HEAD), bf16),
        ],
        scratch_shapes=[pltpu.VMEM((CHIPS, 2, UNIT, HEAD), f32)],
        compiler_params=pltpu.CompilerParams(vmem_limit_bytes=8 << 20),
        name="collect",
    )(slot_prompt, owner, got)


def unkey_kernel(sum_ref, other_ref, units_ref, gain_ref, table_ref, out_ref):
    core, chip = lax.axis_index("core"), lax.axis_index(SPREAD)
    rows = pl.ds(pl.multiple_of(chip * PIECE, PIECE), PIECE)
    cos, sin = cos_sin(table_ref[core, rows])
    total = sum_ref[...] + other_ref[...].astype(f32)
    units = units_ref[...].astype(f32)
    dk, dv = total[:, :PIECE], total[:, PIECE:]
    raw = units[:, UNIT:UNIT + PIECE] + units[:, UNIT + PIECE:]
    inv = lax.rsqrt(jnp.mean(raw * raw, axis=-1, keepdims=True) + EPS)
    turned = swap_halves((dk * sin).reshape(HALF, HEAD)).reshape(CHIPS, PIECE, HEAD)
    dn = (dk * cos + turned) * gain_ref[...]
    dot = jnp.mean(raw * dn, axis=-1, keepdims=True)
    d_raw = inv * (dn - raw * (inv * inv * dot))
    out_ref[...] = jnp.concatenate(
        [d_raw.reshape(HALF, HEAD), dv.reshape(HALF, HEAD)], axis=1
    ).astype(bf16)


def unkey(sums, other, units, gain, table):
    vmem = pl.BlockSpec(memory_space=pltpu.VMEM)
    return pl.pallas_call(
        unkey_kernel,
        in_specs=[vmem] * 5,
        out_specs=vmem,
        out_shape=jax.ShapeDtypeStruct((HALF, 2 * HEAD), bf16),
        compiler_params=pltpu.CompilerParams(vmem_limit_bytes=8 << 20),
        name="unkey",
    )(sums, other, units, gain, table)


def input_grad_kernel(wk_ref, wv_ref, *refs):
    grads, got, out_ref = refs[:Y], refs[Y:2 * Y - 1], refs[-1]
    y = lax.axis_index("y")
    for half in range(X_LO):
        rows = pl.ds(pl.multiple_of((half * Y + y) * COLS, COLS), COLS)
        total = dot_nt(grads[0][...], jnp.concatenate([wk_ref[rows], wv_ref[rows]], axis=1))
        for k in range(1, Y):
            w = jnp.concatenate([got[k - 1][half, 0], got[k - 1][half, 1]], axis=1)
            total += dot_nt(grads[k][...], w)
        out_ref[:, half] = total.reshape(CHIPS, PIECE, COLS).astype(bf16)


def input_grad(wk, wv, grads, got):
    vmem = pl.BlockSpec(memory_space=pltpu.VMEM)
    return pl.pallas_call(
        input_grad_kernel,
        in_specs=[vmem] * (2 * Y + 1),
        out_specs=vmem,
        out_shape=jax.ShapeDtypeStruct((CHIPS, X_LO, PIECE, COLS), bf16),
        compiler_params=pltpu.CompilerParams(vmem_limit_bytes=16 << 20),
        cost_estimate=pl.CostEstimate(flops=2 * HALF * WIDTH * 256, bytes_accessed=4 << 20, transcendentals=0),
        name="input_grad",
    )(wk, wv, *grads, *got)


def together(first, second):
    flat, tree = jax.tree.flatten((first, second))
    return jax.tree.unflatten(tree, lax.optimization_barrier(flat))


def swap_y(x, k):
    return lax.ppermute(x, "y", [(i, i ^ k) for i in range(Y)])


def spread(x):
    return lax.all_to_all(x, SPREAD, 0, 0, tiled=True)


def swap_cores(x):
    return lax.ppermute(x, "core", [(0, 1), (1, 0)])


def on_device(
    prompt_x, key_matrix, value_matrix, k_gain, queries, response_keys, response_values,
    output_gradient, response_counts, slot_prompt, prompt_owner, prompt_lengths,
):
    table = rope_table()
    gain = k_gain.reshape(1, HEAD)
    with jax.named_scope("keys_out"):
        units, *send = project(prompt_x, key_matrix, value_matrix, gain, table)
        got = [swap_y(send[k - 1], k) for k in range(1, Y)]
        mine = spread(units)
        needed = select(slot_prompt, prompt_owner, mine, swap_cores(mine))
        needed, (got[0], got[2]) = together(spread(needed), (got[0], got[2]))
    with jax.named_scope("attention"):
        dq, drk, drv, grads = attend(
            response_counts, slot_prompt, prompt_lengths,
            needed, queries, output_gradient, response_keys, response_values,
        )
    with jax.named_scope("grads_back"):
        sums, other = collect(slot_prompt, prompt_owner, spread(grads))
        other, got[1] = together(other, got[1])
        both = unkey(sums, swap_cores(other), mine, gain, table)
        both = [both] + [swap_y(both, k) for k in range(1, Y)]
    with jax.named_scope("input_grad"):
        shares = input_grad(key_matrix, value_matrix, both, got)
        shares = shares.reshape(CHIPS * X_LO, PIECE, COLS)
        shares = lax.all_to_all(shares, SPREAD + ("x_lo",), 0, 0, tiled=True)
        shares = shares.reshape(CHIPS, X_LO, PIECE, COLS).astype(f32)
        d_prompt = jnp.sum(shares, axis=1).reshape(HALF, COLS).astype(bf16)
    return dq, drk, drv, d_prompt


def solution(mesh):
    fine = Mesh(mesh.devices.reshape(2, 8, 2, 2, 4), ("x_hi", "z", "core", "x_lo", "y"))
    dp, tensor = ("x_hi", "z", "core"), ("x_lo", "y")
    both = P(dp, tensor)
    return jax.shard_map(
        on_device,
        mesh=fine,
        in_specs=(P(dp, None), P(None, tensor), P(None, tensor), P(), both, both, both, both, P(), P(), P(), P()),
        out_specs=(both,) * 4,
        check_vma=False,
    )
```

profile of v0, /device:TPU:32, one launch (start us, length us, event | category | flops | bytes accessed | tf_op | source)
XLA Modules:
  0.0 95.9 jit_solution(5711250287242214364)
XLA Ops:
  0.6 0.0 copy-start.4
  0.6 0.0 copy-start.5
  0.7 4.4 %project.1 = (bf16[16,32,128]{2,1,0:T(8,128)(2,1)}, bf16[2,2,640,128]{3,2,1,0:T(8,128)(2,1)}, bf16[2,2,640,128]{3,2,1,0:T(8,128)(2,1)}, bf16[2,2,640,128]{3,2,1,0:T(8,128)(2,1)}) custom-call(bf16[128,5120]{1,0:T(8,128)(2,1)} %x_ref.1, bf16[5120,128]{1,0:T(8,128)(2,1)} %wk_ref.3, bf16[5120,128]{1,0:T(8,128)(2,1)} %wv_ref.3, f32[1,128]{1,0:T(1,128)} %bitcast.9, ...), custom_call_target="tpu_custom_call" | custom-call | flops 335544320 | bytes 4194304 | tf_op jit(solution)/shard_map/keys_out/project/pallas_call | solution.py:129
  5.1 0.0 copy-start.6
  5.1 0.0 copy-start.7
  5.1 0.0 copy-start.8
  5.1 0.0 copy-start.9
  5.1 0.0 copy-start.10
  5.1 0.0 copy-start.11
  5.2 11.2 %all-to-all-start = ((bf16[16,32,128]{2,1,0:T(8,128)(2,1)}), bf16[16,32,128]{2,1,0:T(8,128)(2,1)S(1)}, u32[]{:S(2)}, u32[]{:S(2)}) async-start(bf16[16,32,128]{2,1,0:T(8,128)(2,1)} %get-tuple-element.19), calls=%async_computation | async-start | bytes 262144 | tf_op jit(solution)/shard_map/keys_out/all_to_all | solution.py:356
  16.3 1.6 %collective-permute-start.1 = (bf16[2,2,640,128]{3,2,1,0:T(8,128)(2,1)}, bf16[2,2,640,128]{3,2,1,0:T(8,128)(2,1)S(1)}, u32[]{:S(2)}, u32[]{:S(2)}) collective-permute-start(bf16[2,2,640,128]{3,2,1,0:T(8,128)(2,1)} %get-tuple-element.20), channel_id=1, source_target_pairs={{0,1},{1,0},{2,3},{3,2},{4,5},{5,4},{6,7},{7,6},{8,9},{9,8},{10,11... | collective-permute-start | bytes 1966088 | tf_op jit(solution)/shard_map/keys_out/ppermute | solution.py:352
  17.9 2.2 %collective-permute-start.2 = (bf16[2,2,640,128]{3,2,1,0:T(8,128)(2,1)}, bf16[2,2,640,128]{3,2,1,0:T(8,128)(2,1)S(1)}, u32[]{:S(2)}, u32[]{:S(2)}) collective-permute-start(bf16[2,2,640,128]{3,2,1,0:T(8,128)(2,1)} %get-tuple-element.21), channel_id=1, source_target_pairs={{0,3},{1,2},{2,1},{3,0},{4,7},{5,6},{6,5},{7,4},{8,11},{9,10},{10,... | collective-permute-start | bytes 1966088 | tf_op jit(solution)/shard_map/keys_out/ppermute | solution.py:352
  20.1 5.8 %all-to-all-done.mine_ref.units_ref = bf16[16,32,128]{2,1,0:T(8,128)(2,1)S(1)} async-done(((bf16[16,32,128]{2,1,0:T(8,128)(2,1)}), bf16[16,32,128]{2,1,0:T(8,128)(2,1)S(1)}, u32[]{:S(2)}, u32[]{:S(2)}) %all-to-all-start) | async-done | bytes 131104 | tf_op jit(solution)/shard_map/keys_out/all_to_all | solution.py:356
  25.9 0.0 collective-permute-start
  26.0 1.3 %collective-permute-done.other_ref = bf16[16,32,128]{2,1,0:T(8,128)(2,1)S(1)} collective-permute-done((bf16[16,32,128]{2,1,0:T(8,128)(2,1)S(1)}, bf16[16,32,128]{2,1,0:T(8,128)(2,1)S(1)}, u32[]{:S(2)}, u32[]{:S(2)}) %collective-permute-start) | collective-permute-done | bytes 131104 | tf_op jit(solution)/shard_map/keys_out/ppermute | solution.py:360
  27.3 0.0 copy-done.4
  27.3 0.0 copy-done.5
  27.3 1.3 %select.1 = bf16[16,2,2,16,128]{4,3,2,1,0:T(8,128)(2,1)} custom-call(s32[64]{0:T(128)S(1)} %copy-done.4, s32[16]{0:T(128)S(1)} %copy-done.5, bf16[16,32,128]{2,1,0:T(8,128)(2,1)S(1)} %all-to-all-done.mine_ref.units_ref, bf16[16,32,128]{2,1,0:T(8,128)(2,1)S(1)} %collective-permute-done.other_ref), custom_call_target="tpu_custom_call" | custom-call | tf_op jit(solution)/shard_map/keys_out/select/pallas_call | solution.py:160
  28.6 3.9 %all-to-all-start.1 = ((bf16[16,2,2,16,128]{4,3,2,1,0:T(8,128)(2,1)}), bf16[16,2,2,16,128]{4,3,2,1,0:T(8,128)(2,1)S(1)}, u32[]{:S(2)}, u32[]{:S(2)}) async-start(bf16[16,2,2,16,128]{4,3,2,1,0:T(8,128)(2,1)} %select.1), calls=%async_computation.1 | async-start | bytes 524288 | tf_op jit(solution)/shard_map/keys_out/all_to_all | solution.py:356
  32.5 3.2 %collective-permute-start.3 = (bf16[2,2,640,128]{3,2,1,0:T(8,128)(2,1)}, bf16[2,2,640,128]{3,2,1,0:T(8,128)(2,1)S(1)}, u32[]{:S(2)}, u32[]{:S(2)}) collective-permute-start(bf16[2,2,640,128]{3,2,1,0:T(8,128)(2,1)} %get-tuple-element.29), channel_id=1, source_target_pairs={{0,2},{1,3},{2,0},{3,1},{4,6},{5,7},{6,4},{7,5},{8,10},{9,11},{10,... | collective-permute-start | bytes 1966088 | tf_op jit(solution)/shard_map/keys_out/ppermute | solution.py:352
  35.7 0.0 collective-permute-done.1.refs_4_
  35.7 0.0 collective-permute-done.2.refs_6_
  35.7 9.0 %all-to-all-done.1.kv_ref = bf16[16,2,2,16,128]{4,3,2,1,0:T(8,128)(2,1)S(1)} async-done(((bf16[16,2,2,16,128]{4,3,2,1,0:T(8,128)(2,1)}), bf16[16,2,2,16,128]{4,3,2,1,0:T(8,128)(2,1)S(1)}, u32[]{:S(2)}, u32[]{:S(2)}) %all-to-all-start.1) | async-done | bytes 262176 | tf_op jit(solution)/shard_map/keys_out/all_to_all | solution.py:356
  44.7 0.0 copy-done.6
  44.7 0.0 copy-done.7
  44.7 0.0 copy-done.8
  44.7 0.0 copy-done.9
  44.8 0.0 copy-done.10
  44.8 0.0 copy-done.11
  44.8 0.0 copy-start.2
  44.8 0.0 copy-start.3
  44.8 0.0 copy-start.1
  44.8 4.6 %attend.1 = (bf16[256,1024]{1,0:T(8,128)(2,1)}, bf16[256,128]{1,0:T(8,128)(2,1)}, bf16[256,128]{1,0:T(8,128)(2,1)}, bf16[16,2,2,16,128]{4,3,2,1,0:T(8,128)(2,1)S(1)}) custom-call(s32[1,32]{1,0:T(1,128)S(1)} %bitcast.12, s32[1,64]{1,0:T(1,128)S(1)} %bitcast.11, s32[1,16]{1,0:T(1,128)S(1)} %bitcast.13, bf16[16,2,2,16,128]{4,3,2,1,0:T(8,128)(2,1)S(1)} %all-to-all-done.1.kv_ref, ...), custom_call_target="tpu_custom_call" | custom-call | flops 1006632960 | bytes 3145728 | tf_op jit(solution)/shard_map/attention/attend/pallas_call | solution.py:244
  49.4 0.0 copy-start
  49.4 16.1 %all_to_all.20.got_ref = bf16[16,2,2,16,128]{4,3,2,1,0:T(8,128)(2,1)S(1)} all-to-all(bf16[16,2,2,16,128]{4,3,2,1,0:T(8,128)(2,1)S(1)} %get-tuple-element.26), channel_id=1, replica_groups=mesh['x_hi'=2,'z'=8,'core'=2,'x_lo'=2,'y'=4] {'x_hi','z'}, dimensions={0} | all-to-all | bytes 524288 | tf_op jit(solution)/shard_map/grads_back/all_to_all | solution.py:356
  65.5 0.7 collect.1
  66.2 0.0 collective-permute-done.3.refs_5_
  66.2 0.1 collective-permute-start.4
  66.3 1.2 %collective-permute-done.4.other_ref = bf16[16,16,128]{2,1,0:T(8,128)(2,1)S(1)} collective-permute-done((bf16[16,16,128]{2,1,0:T(8,128)(2,1)S(1)}, bf16[16,16,128]{2,1,0:T(8,128)(2,1)S(1)}, u32[]{:S(2)}, u32[]{:S(2)}) %collective-permute-start.4) | collective-permute-done | bytes 65568 | tf_op jit(solution)/shard_map/grads_back/ppermute | solution.py:360
  67.5 0.0 copy-done.2
  67.5 0.0 copy-done.3
  67.5 0.2 unkey.1.refs_0_
  67.8 3.1 %collective-permute-start.7 = (bf16[128,256]{1,0:T(8,128)(2,1)S(1)}, bf16[128,256]{1,0:T(8,128)(2,1)S(1)}, u32[]{:S(2)}, u32[]{:S(2)}) collective-permute-start(bf16[128,256]{1,0:T(8,128)(2,1)S(1)} %unkey.1.refs_0_), channel_id=1, source_target_pairs={{0,3},{1,2},{2,1},{3,0},{4,7},{5,6},{6,5},{7,4},{8,11},{9,10},{10,... | collective-permute-start | bytes 196616 | tf_op jit(solution)/shard_map/grads_back/ppermute | solution.py:352
  70.9 0.5 collective-permute-start.6
  71.4 0.6 collective-permute-start.5
  72.0 2.0 %collective-permute-done.7.refs_3_ = bf16[128,256]{1,0:T(8,128)(2,1)S(1)} collective-permute-done((bf16[128,256]{1,0:T(8,128)(2,1)S(1)}, bf16[128,256]{1,0:T(8,128)(2,1)S(1)}, u32[]{:S(2)}, u32[]{:S(2)}) %collective-permute-start.7) | collective-permute-done | bytes 65568 | tf_op jit(solution)/shard_map/grads_back/ppermute | solution.py:352
  74.0 3.0 %collective-permute-done.6.refs_2_ = bf16[128,256]{1,0:T(8,128)(2,1)S(1)} collective-permute-done((bf16[128,256]{1,0:T(8,128)(2,1)S(1)}, bf16[128,256]{1,0:T(8,128)(2,1)S(1)}, u32[]{:S(2)}, u32[]{:S(2)}) %collective-permute-start.6) | collective-permute-done | bytes 65568 | tf_op jit(solution)/shard_map/grads_back/ppermute | solution.py:352
  77.0 0.0 collective-permute-done.5.refs_1_
  77.0 0.0 copy-done.1
  77.0 0.0 copy-done
  77.0 0.9 input_grad.1
  77.9 17.3 %all_to_all.21 = bf16[32,8,640]{2,1,0:T(8,128)(2,1)S(1)} all-to-all(bf16[32,8,640]{2,1,0:T(8,128)(2,1)S(1)} %bitcast.8), channel_id=1, replica_groups=mesh['x_hi'=2,'z'=8,'core'=2,'x_lo'=2,'y'=4] {'x_hi','z','x_lo'}, dimensions={0} | all-to-all | bytes 655360 | tf_op jit(solution)/shard_map/input_grad/all_to_all | solution.py:388
  95.2 0.7 bitcast_reduce_fusion
Async XLA Ops:
  0.6 26.7 %copy-start.4 = (s32[64]{0:T(128)S(1)}, s32[64]{0:T(128)}, u32[]{:S(2)}) copy-start(s32[64]{0:T(128)} %slot_prompt_ref.3) | copy-start | bytes 772
  0.6 26.7 %copy-start.5 = (s32[16]{0:T(128)S(1)}, s32[16]{0:T(128)}, u32[]{:S(2)}) copy-start(s32[16]{0:T(128)} %owner_ref.3) | copy-start | bytes 196
  5.1 39.7 %copy-start.6 = (bf16[256,1024]{1,0:T(8,128)(2,1)S(1)}, bf16[256,1024]{1,0:T(8,128)(2,1)}, u32[]{:S(2)}) copy-start(bf16[256,1024]{1,0:T(8,128)(2,1)} %q_ref.1) | copy-start | bytes 1572868
  5.1 39.6 %copy-start.7 = (bf16[256,1024]{1,0:T(8,128)(2,1)S(1)}, bf16[256,1024]{1,0:T(8,128)(2,1)}, u32[]{:S(2)}) copy-start(bf16[256,1024]{1,0:T(8,128)(2,1)} %g_ref.1) | copy-start | bytes 1572868
  5.1 39.6 %copy-start.8 = (bf16[256,128]{1,0:T(8,128)(2,1)S(1)}, bf16[256,128]{1,0:T(8,128)(2,1)}, u32[]{:S(2)}) copy-start(bf16[256,128]{1,0:T(8,128)(2,1)} %rk_ref.1) | copy-start | bytes 196612
  5.1 39.6 %copy-start.9 = (bf16[256,128]{1,0:T(8,128)(2,1)S(1)}, bf16[256,128]{1,0:T(8,128)(2,1)}, u32[]{:S(2)}) copy-start(bf16[256,128]{1,0:T(8,128)(2,1)} %rv_ref.1) | copy-start | bytes 196612
  5.1 39.6 %copy-start.10 = (s32[32]{0:T(128)S(1)}, s32[32]{0:T(128)}, u32[]{:S(2)}) copy-start(s32[32]{0:T(128)} %param.21) | copy-start | bytes 388
  5.1 39.6 %copy-start.11 = (s32[16]{0:T(128)S(1)}, s32[16]{0:T(128)}, u32[]{:S(2)}) copy-start(s32[16]{0:T(128)} %param.24) | copy-start | bytes 196
  5.2 20.8 %all-to-all-start = ((bf16[16,32,128]{2,1,0:T(8,128)(2,1)}), bf16[16,32,128]{2,1,0:T(8,128)(2,1)S(1)}, u32[]{:S(2)}, u32[]{:S(2)}) async-start(bf16[16,32,128]{2,1,0:T(8,128)(2,1)} %get-tuple-element.19), calls=%async_computation | async-start | bytes 262144 | tf_op jit(solution)/shard_map/keys_out/all_to_all | solution.py:356
  16.3 19.4 %collective-permute-start.1 = (bf16[2,2,640,128]{3,2,1,0:T(8,128)(2,1)}, bf16[2,2,640,128]{3,2,1,0:T(8,128)(2,1)S(1)}, u32[]{:S(2)}, u32[]{:S(2)}) collective-permute-start(bf16[2,2,640,128]{3,2,1,0:T(8,128)(2,1)} %get-tuple-element.20), channel_id=1, source_target_pairs={{0,1},{1,0},{2,3},{3,2},{4,5},{5,4},{6,7},{7,6},{8,9},{9,8},{10,11... | collective-permute-start | bytes 1966088 | tf_op jit(solution)/shard_map/keys_out/ppermute | solution.py:352
  17.9 17.8 %collective-permute-start.2 = (bf16[2,2,640,128]{3,2,1,0:T(8,128)(2,1)}, bf16[2,2,640,128]{3,2,1,0:T(8,128)(2,1)S(1)}, u32[]{:S(2)}, u32[]{:S(2)}) collective-permute-start(bf16[2,2,640,128]{3,2,1,0:T(8,128)(2,1)} %get-tuple-element.21), channel_id=1, source_target_pairs={{0,3},{1,2},{2,1},{3,0},{4,7},{5,6},{6,5},{7,4},{8,11},{9,10},{10,... | collective-permute-start | bytes 1966088 | tf_op jit(solution)/shard_map/keys_out/ppermute | solution.py:352
  25.9 1.3 %collective-permute-start = (bf16[16,32,128]{2,1,0:T(8,128)(2,1)S(1)}, bf16[16,32,128]{2,1,0:T(8,128)(2,1)S(1)}, u32[]{:S(2)}, u32[]{:S(2)}) collective-permute-start(bf16[16,32,128]{2,1,0:T(8,128)(2,1)S(1)} %all-to-all-done.mine_ref.units_ref), channel_id=1, source_target_pairs={{0,8},{8,0},{1,9},{9,1},{2,10},{10,2},{3,11},{11,3},{4,12},{12,4},... | collective-permute-start | bytes 393224 | tf_op jit(solution)/shard_map/keys_out/ppermute | solution.py:360
  28.6 16.1 %all-to-all-start.1 = ((bf16[16,2,2,16,128]{4,3,2,1,0:T(8,128)(2,1)}), bf16[16,2,2,16,128]{4,3,2,1,0:T(8,128)(2,1)S(1)}, u32[]{:S(2)}, u32[]{:S(2)}) async-start(bf16[16,2,2,16,128]{4,3,2,1,0:T(8,128)(2,1)} %select.1), calls=%async_computation.1 | async-start | bytes 524288 | tf_op jit(solution)/shard_map/keys_out/all_to_all | solution.py:356
  32.5 33.7 %collective-permute-start.3 = (bf16[2,2,640,128]{3,2,1,0:T(8,128)(2,1)}, bf16[2,2,640,128]{3,2,1,0:T(8,128)(2,1)S(1)}, u32[]{:S(2)}, u32[]{:S(2)}) collective-permute-start(bf16[2,2,640,128]{3,2,1,0:T(8,128)(2,1)} %get-tuple-element.29), channel_id=1, source_target_pairs={{0,2},{1,3},{2,0},{3,1},{4,6},{5,7},{6,4},{7,5},{8,10},{9,11},{10,... | collective-permute-start | bytes 1966088 | tf_op jit(solution)/shard_map/keys_out/ppermute | solution.py:352
  44.8 22.8 %copy-start.2 = (f32[2,128,128]{2,1,0:T(8,128)S(1)}, f32[2,128,128]{2,1,0:T(8,128)}, u32[]{:S(2)}) copy-start(f32[2,128,128]{2,1,0:T(8,128)} %constant.4.clone.table_ref) | copy-start | bytes 393220
  44.8 22.8 %copy-start.3 = (f32[128]{0:T(128)S(1)}, f32[128]{0:T(128)}, u32[]{:S(2)}) copy-start(f32[128]{0:T(128)} %param.16) | copy-start | bytes 1540
  44.8 32.2 %copy-start.1 = (bf16[5120,128]{1,0:T(8,128)(2,1)S(1)}, bf16[5120,128]{1,0:T(8,128)(2,1)}, u32[]{:S(2)}) copy-start(bf16[5120,128]{1,0:T(8,128)(2,1)} %wv_ref.3) | copy-start | bytes 3932164
  49.4 27.6 %copy-start = (bf16[5120,128]{1,0:T(8,128)(2,1)S(1)}, bf16[5120,128]{1,0:T(8,128)(2,1)}, u32[]{:S(2)}) copy-start(bf16[5120,128]{1,0:T(8,128)(2,1)} %wk_ref.3) | copy-start | bytes 3932164
  66.2 1.3 %collective-permute-start.4 = (bf16[16,16,128]{2,1,0:T(8,128)(2,1)S(1)}, bf16[16,16,128]{2,1,0:T(8,128)(2,1)S(1)}, u32[]{:S(2)}, u32[]{:S(2)}) collective-permute-start(bf16[16,16,128]{2,1,0:T(8,128)(2,1)S(1)} %get-tuple-element.30), channel_id=1, source_target_pairs={{0,8},{8,0},{1,9},{9,1},{2,10},{10,2},{3,11},{11,3},{4,12},{12,4},... | collective-permute-start | bytes 196616 | tf_op jit(solution)/shard_map/grads_back/ppermute | solution.py:360
  67.8 6.2 %collective-permute-start.7 = (bf16[128,256]{1,0:T(8,128)(2,1)S(1)}, bf16[128,256]{1,0:T(8,128)(2,1)S(1)}, u32[]{:S(2)}, u32[]{:S(2)}) collective-permute-start(bf16[128,256]{1,0:T(8,128)(2,1)S(1)} %unkey.1.refs_0_), channel_id=1, source_target_pairs={{0,3},{1,2},{2,1},{3,0},{4,7},{5,6},{6,5},{7,4},{8,11},{9,10},{10,... | collective-permute-start | bytes 196616 | tf_op jit(solution)/shard_map/grads_back/ppermute | solution.py:352
  70.9 6.1 %collective-permute-start.6 = (bf16[128,256]{1,0:T(8,128)(2,1)S(1)}, bf16[128,256]{1,0:T(8,128)(2,1)S(1)}, u32[]{:S(2)}, u32[]{:S(2)}) collective-permute-start(bf16[128,256]{1,0:T(8,128)(2,1)S(1)} %unkey.1.refs_0_), channel_id=1, source_target_pairs={{0,2},{1,3},{2,0},{3,1},{4,6},{5,7},{6,4},{7,5},{8,10},{9,11},{10,... | collective-permute-start | bytes 196616 | tf_op jit(solution)/shard_map/grads_back/ppermute | solution.py:352
  71.4 5.6 %collective-permute-start.5 = (bf16[128,256]{1,0:T(8,128)(2,1)S(1)}, bf16[128,256]{1,0:T(8,128)(2,1)S(1)}, u32[]{:S(2)}, u32[]{:S(2)}) collective-permute-start(bf16[128,256]{1,0:T(8,128)(2,1)S(1)} %unkey.1.refs_0_), channel_id=1, source_target_pairs={{0,1},{1,0},{2,3},{3,2},{4,5},{5,4},{6,7},{7,6},{8,9},{9,8},{10,11... | collective-permute-start | bytes 196616 | tf_op jit(solution)/shard_map/grads_back/ppermute | solution.py:352
where the time goes:
time: 96.5 us; the launch traced here: 95.9 us
  blocking collectives  33.4 us (35%)
  starting transfers between devices  26.3 us (27%)
  waiting for transfers between devices  22.5 us (23%)
  Pallas kernels  12.1 us (13%)
    all_to_all x1, blocking collectives, on_device(): shares = lax.all_to_all(shares, SPREAD + ('x_lo',), 0, 0, tiled=True)  17.3 us
    all_to_all x1, blocking collectives, spread(): return lax.all_to_all(x, SPREAD, 0, 0, tiled=True)  16.1 us
    all_to_all x2, starting transfers between devices, spread(): return lax.all_to_all(x, SPREAD, 0, 0, tiled=True)  15.1 us
    all_to_all x2, waiting for transfers between devices, spread(): return lax.all_to_all(x, SPREAD, 0, 0, tiled=True)  14.9 us
    ppermute x6, starting transfers between devices, swap_y(): return lax.ppermute(x, 'y', [(i, i ^ k) for i in range(Y)])  11.1 us
    ppermute x6, waiting for transfers between devices, swap_y(): return lax.ppermute(x, 'y', [(i, i ^ k) for i in range(Y)])  5.01 us
    pallas_call x1, Pallas kernels, attend(): pl.pallas_call(attend_kernel, in_specs=[vmem] * 8, out_specs=[vmem] * 4,...  4.55 us
    pallas_call x1, Pallas kernels, project(): pl.pallas_call(project_kernel, in_specs=[hbm, hbm, hbm, vmem, hbm], out_s...  4.43 us
  transfers between devices with their start and end apart: 10, of which 6 were waited for; matrix products, arithmetic and copies ran while one was open for 0% of the time, Pallas kernels for 7%

commit v1 on v0

--- a/solution.py
+++ b/solution.py
@@ -78,7 +78,7 @@
 def project_kernel(
     x_ref, wk_ref, wv_ref, gain_ref, table_ref, units_ref, *refs
 ):
-    send_refs, (x_s, w_s, table_s, sems, table_sem, send_sems) = refs[:Y - 1], refs[Y - 1:]
+    send_refs, (x_s, w_s, table_s, gain_s, sems, small_sems, send_sems) = refs[:Y - 1], refs[Y - 1:]
     core, y = lax.axis_index("core"), lax.axis_index("y")
     order = [(k, half) for k in range(1, Y) for half in range(X_LO)] + [(0, 0), (0, 1)]
     copies = []
@@ -93,8 +93,12 @@
         )
         for copy in copies[-1]:
             copy.start()
-    table = pltpu.make_async_copy(table_ref.at[core], table_s, table_sem)
-    table.start()
+    small = [
+        pltpu.make_async_copy(table_ref.at[core], table_s, small_sems.at[0]),
+        pltpu.make_async_copy(gain_ref, gain_s, small_sems.at[1]),
+    ]
+    for copy in small:
+        copy.start()
     sends = [
         pltpu.make_async_copy(w_s.at[n], send_refs[k - 1].at[half], send_sems.at[n])
         for n, (k, half) in enumerate(order)
@@ -107,11 +111,12 @@
         if n < len(sends):
             sends[n].start()
         acc += dot_nn(x_s[n], jnp.concatenate([w_s[n, 0], w_s[n, 1]], axis=1))
-    table.wait()
+    for copy in small:
+        copy.wait()
     cos, sin = cos_sin(table_s[...])
     raw = acc[:, :HEAD]
     inv = lax.rsqrt(jnp.mean(raw * raw, axis=-1, keepdims=True) + EPS)
-    u = raw * inv * gain_ref[...]
+    u = raw * inv * gain_s[...]
     keys = u * cos + swap_halves(u) * sin
     high = raw.astype(bf16).astype(f32)
     parts = [keys, acc[:, HEAD:], high, raw - high]
@@ -128,7 +133,7 @@
     anywhere = pl.BlockSpec(memory_space=pl.ANY)
     return pl.pallas_call(
         project_kernel,
-        in_specs=[hbm, hbm, hbm, vmem, hbm],
+        in_specs=[hbm] * 5,
         out_specs=[vmem] + [anywhere] * (Y - 1),
         out_shape=[jax.ShapeDtypeStruct((CHIPS, 2 * UNIT, HEAD), bf16)]
         + [jax.ShapeDtypeStruct((X_LO, 2, COLS, HEAD), bf16)] * (Y - 1),
@@ -136,8 +141,9 @@
             pltpu.VMEM((TENSOR, HALF, COLS), bf16),
             pltpu.VMEM((TENSOR, 2, COLS, HEAD), bf16),
             pltpu.VMEM((HALF, HEAD), f32),
+            pltpu.VMEM((1, HEAD), f32),
             pltpu.SemaphoreType.DMA((TENSOR, 3)),
-            pltpu.SemaphoreType.DMA(()),
+            pltpu.SemaphoreType.DMA((2,)),
             pltpu.SemaphoreType.DMA((TENSOR - X_LO,)),
         ],
         compiler_params=pltpu.CompilerParams(vmem_limit_bytes=PROJECT_VMEM),

time: 96.5 us -> 95.9 us (level)
  no operation moved by 1% of the time
where the time goes in v1:
time: 95.9 us; the launch traced here: 95.3 us
  blocking collectives  33.4 us (35%)
  starting transfers between devices  26.3 us (27%)
  waiting for transfers between devices  22.4 us (23%)
  Pallas kernels  11.5 us (12%)
    all_to_all x1, blocking collectives, on_device(): shares = lax.all_to_all(shares, SPREAD + ('x_lo',), 0, 0, tiled=True)  17.3 us
    all_to_all x1, blocking collectives, spread(): return lax.all_to_all(x, SPREAD, 0, 0, tiled=True)  16.1 us
    all_to_all x2, starting transfers between devices, spread(): return lax.all_to_all(x, SPREAD, 0, 0, tiled=True)  15.1 us
    all_to_all x2, waiting for transfers between devices, spread(): return lax.all_to_all(x, SPREAD, 0, 0, tiled=True)  14.9 us
    ppermute x6, starting transfers between devices, swap_y(): return lax.ppermute(x, 'y', [(i, i ^ k) for i in range(Y)])  11.1 us
    ppermute x6, waiting for transfers between devices, swap_y(): return lax.ppermute(x, 'y', [(i, i ^ k) for i in range(Y)])  5 us
    pallas_call x1, Pallas kernels, attend(): pl.pallas_call(attend_kernel, in_specs=[vmem] * 8, out_specs=[vmem] * 4,...  4.55 us
    pallas_call x1, Pallas kernels, project(): pl.pallas_call(project_kernel, in_specs=[hbm] * 5, out_specs=[vmem] + [an...  3.84 us
  transfers between devices with their start and end apart: 10, of which 6 were waited for; matrix products, arithmetic and copies ran while one was open for 0% of the time, Pallas kernels for 7%

profile of v1, /device:TPU:32, one launch (start us, length us, event | category | flops | bytes accessed | tf_op | source)
XLA Modules:
  0.0 95.3 jit_solution(705013155293140464)
XLA Ops:
  0.6 0.0 copy-start.4
  0.6 0.0 copy-start.5
  0.7 3.8 %project.1 = (bf16[16,32,128]{2,1,0:T(8,128)(2,1)}, bf16[2,2,640,128]{3,2,1,0:T(8,128)(2,1)}, bf16[2,2,640,128]{3,2,1,0:T(8,128)(2,1)}, bf16[2,2,640,128]{3,2,1,0:T(8,128)(2,1)}) custom-call(bf16[128,5120]{1,0:T(8,128)(2,1)} %x_ref.1, bf16[5120,128]{1,0:T(8,128)(2,1)} %wk_ref.3, bf16[5120,128]{1,0:T(8,128)(2,1)} %wv_ref.3, f32[1,128]{1,0:T(1,128)} %bitcast.9, ...), custom_call_target="tpu_custom_call" | custom-call | flops 335544320 | bytes 4194304 | tf_op jit(solution)/shard_map/keys_out/project/pallas_call | solution.py:134
  4.5 0.0 copy-start.6
  4.5 0.0 copy-start.7
  4.5 0.0 copy-start.8
  4.5 0.0 copy-start.9
  4.5 0.0 copy-start.10
  4.6 0.0 copy-start.11
  4.6 11.2 %all-to-all-start = ((bf16[16,32,128]{2,1,0:T(8,128)(2,1)}), bf16[16,32,128]{2,1,0:T(8,128)(2,1)S(1)}, u32[]{:S(2)}, u32[]{:S(2)}) async-start(bf16[16,32,128]{2,1,0:T(8,128)(2,1)} %get-tuple-element.19), calls=%async_computation | async-start | bytes 262144 | tf_op jit(solution)/shard_map/keys_out/all_to_all | solution.py:362
  15.8 1.6 %collective-permute-start.1 = (bf16[2,2,640,128]{3,2,1,0:T(8,128)(2,1)}, bf16[2,2,640,128]{3,2,1,0:T(8,128)(2,1)S(1)}, u32[]{:S(2)}, u32[]{:S(2)}) collective-permute-start(bf16[2,2,640,128]{3,2,1,0:T(8,128)(2,1)} %get-tuple-element.20), channel_id=1, source_target_pairs={{0,1},{1,0},{2,3},{3,2},{4,5},{5,4},{6,7},{7,6},{8,9},{9,8},{10,11... | collective-permute-start | bytes 1966088 | tf_op jit(solution)/shard_map/keys_out/ppermute | solution.py:358
  17.3 2.2 %collective-permute-start.2 = (bf16[2,2,640,128]{3,2,1,0:T(8,128)(2,1)}, bf16[2,2,640,128]{3,2,1,0:T(8,128)(2,1)S(1)}, u32[]{:S(2)}, u32[]{:S(2)}) collective-permute-start(bf16[2,2,640,128]{3,2,1,0:T(8,128)(2,1)} %get-tuple-element.21), channel_id=1, source_target_pairs={{0,3},{1,2},{2,1},{3,0},{4,7},{5,6},{6,5},{7,4},{8,11},{9,10},{10,... | collective-permute-start | bytes 1966088 | tf_op jit(solution)/shard_map/keys_out/ppermute | solution.py:358
  19.5 5.8 %all-to-all-done.mine_ref.units_ref = bf16[16,32,128]{2,1,0:T(8,128)(2,1)S(1)} async-done(((bf16[16,32,128]{2,1,0:T(8,128)(2,1)}), bf16[16,32,128]{2,1,0:T(8,128)(2,1)S(1)}, u32[]{:S(2)}, u32[]{:S(2)}) %all-to-all-start) | async-done | bytes 131104 | tf_op jit(solution)/shard_map/keys_out/all_to_all | solution.py:362
  25.4 0.0 collective-permute-start
  25.4 1.3 %collective-permute-done.other_ref = bf16[16,32,128]{2,1,0:T(8,128)(2,1)S(1)} collective-permute-done((bf16[16,32,128]{2,1,0:T(8,128)(2,1)S(1)}, bf16[16,32,128]{2,1,0:T(8,128)(2,1)S(1)}, u32[]{:S(2)}, u32[]{:S(2)}) %collective-permute-start) | collective-permute-done | bytes 131104 | tf_op jit(solution)/shard_map/keys_out/ppermute | solution.py:366
  26.7 0.0 copy-done.4
  26.7 0.0 copy-done.5
  26.7 1.3 %select.1 = bf16[16,2,2,16,128]{4,3,2,1,0:T(8,128)(2,1)} custom-call(s32[64]{0:T(128)S(1)} %copy-done.4, s32[16]{0:T(128)S(1)} %copy-done.5, bf16[16,32,128]{2,1,0:T(8,128)(2,1)S(1)} %all-to-all-done.mine_ref.units_ref, bf16[16,32,128]{2,1,0:T(8,128)(2,1)S(1)} %collective-permute-done.other_ref), custom_call_target="tpu_custom_call" | custom-call | tf_op jit(solution)/shard_map/keys_out/select/pallas_call | solution.py:166
  28.0 3.9 %all-to-all-start.1 = ((bf16[16,2,2,16,128]{4,3,2,1,0:T(8,128)(2,1)}), bf16[16,2,2,16,128]{4,3,2,1,0:T(8,128)(2,1)S(1)}, u32[]{:S(2)}, u32[]{:S(2)}) async-start(bf16[16,2,2,16,128]{4,3,2,1,0:T(8,128)(2,1)} %select.1), calls=%async_computation.1 | async-start | bytes 524288 | tf_op jit(solution)/shard_map/keys_out/all_to_all | solution.py:362
  31.9 3.2 %collective-permute-start.3 = (bf16[2,2,640,128]{3,2,1,0:T(8,128)(2,1)}, bf16[2,2,640,128]{3,2,1,0:T(8,128)(2,1)S(1)}, u32[]{:S(2)}, u32[]{:S(2)}) collective-permute-start(bf16[2,2,640,128]{3,2,1,0:T(8,128)(2,1)} %get-tuple-element.29), channel_id=1, source_target_pairs={{0,2},{1,3},{2,0},{3,1},{4,6},{5,7},{6,4},{7,5},{8,10},{9,11},{10,... | collective-permute-start | bytes 1966088 | tf_op jit(solution)/shard_map/keys_out/ppermute | solution.py:358
  35.1 0.0 collective-permute-done.1.refs_4_
  35.1 0.0 collective-permute-done.2.refs_6_
  35.1 9.0 %all-to-all-done.1.kv_ref = bf16[16,2,2,16,128]{4,3,2,1,0:T(8,128)(2,1)S(1)} async-done(((bf16[16,2,2,16,128]{4,3,2,1,0:T(8,128)(2,1)}), bf16[16,2,2,16,128]{4,3,2,1,0:T(8,128)(2,1)S(1)}, u32[]{:S(2)}, u32[]{:S(2)}) %all-to-all-start.1) | async-done | bytes 262176 | tf_op jit(solution)/shard_map/keys_out/all_to_all | solution.py:362
  44.1 0.0 copy-done.6
  44.1 0.0 copy-done.7
  44.1 0.0 copy-done.8
  44.2 0.0 copy-done.9
  44.2 0.0 copy-done.10
  44.2 0.0 copy-done.11
  44.2 0.0 copy-start.2
  44.2 0.0 copy-start.3
  44.2 0.0 copy-start.1
  44.2 4.6 %attend.1 = (bf16[256,1024]{1,0:T(8,128)(2,1)}, bf16[256,128]{1,0:T(8,128)(2,1)}, bf16[256,128]{1,0:T(8,128)(2,1)}, bf16[16,2,2,16,128]{4,3,2,1,0:T(8,128)(2,1)S(1)}) custom-call(s32[1,32]{1,0:T(1,128)S(1)} %bitcast.12, s32[1,64]{1,0:T(1,128)S(1)} %bitcast.11, s32[1,16]{1,0:T(1,128)S(1)} %bitcast.13, bf16[16,2,2,16,128]{4,3,2,1,0:T(8,128)(2,1)S(1)} %all-to-all-done.1.kv_ref, ...), custom_call_target="tpu_custom_call" | custom-call | flops 1006632960 | bytes 3145728 | tf_op jit(solution)/shard_map/attention/attend/pallas_call | solution.py:250
  48.8 0.0 copy-start
  48.8 16.1 %all_to_all.20.got_ref = bf16[16,2,2,16,128]{4,3,2,1,0:T(8,128)(2,1)S(1)} all-to-all(bf16[16,2,2,16,128]{4,3,2,1,0:T(8,128)(2,1)S(1)} %get-tuple-element.26), channel_id=1, replica_groups=mesh['x_hi'=2,'z'=8,'core'=2,'x_lo'=2,'y'=4] {'x_hi','z'}, dimensions={0} | all-to-all | bytes 524288 | tf_op jit(solution)/shard_map/grads_back/all_to_all | solution.py:362
  64.9 0.7 collect.1
  65.6 0.0 collective-permute-done.3.refs_5_
  65.6 0.1 collective-permute-start.4
  65.7 1.2 %collective-permute-done.4.other_ref = bf16[16,16,128]{2,1,0:T(8,128)(2,1)S(1)} collective-permute-done((bf16[16,16,128]{2,1,0:T(8,128)(2,1)S(1)}, bf16[16,16,128]{2,1,0:T(8,128)(2,1)S(1)}, u32[]{:S(2)}, u32[]{:S(2)}) %collective-permute-start.4) | collective-permute-done | bytes 65568 | tf_op jit(solution)/shard_map/grads_back/ppermute | solution.py:366
  66.9 0.0 copy-done.2
  66.9 0.0 copy-done.3
  66.9 0.2 unkey.1.refs_0_
  67.2 3.1 %collective-permute-start.7 = (bf16[128,256]{1,0:T(8,128)(2,1)S(1)}, bf16[128,256]{1,0:T(8,128)(2,1)S(1)}, u32[]{:S(2)}, u32[]{:S(2)}) collective-permute-start(bf16[128,256]{1,0:T(8,128)(2,1)S(1)} %unkey.1.refs_0_), channel_id=1, source_target_pairs={{0,3},{1,2},{2,1},{3,0},{4,7},{5,6},{6,5},{7,4},{8,11},{9,10},{10,... | collective-permute-start | bytes 196616 | tf_op jit(solution)/shard_map/grads_back/ppermute | solution.py:358
  70.3 0.5 collective-permute-start.6
  70.8 0.6 collective-permute-start.5
  71.4 2.0 %collective-permute-done.7.refs_3_ = bf16[128,256]{1,0:T(8,128)(2,1)S(1)} collective-permute-done((bf16[128,256]{1,0:T(8,128)(2,1)S(1)}, bf16[128,256]{1,0:T(8,128)(2,1)S(1)}, u32[]{:S(2)}, u32[]{:S(2)}) %collective-permute-start.7) | collective-permute-done | bytes 65568 | tf_op jit(solution)/shard_map/grads_back/ppermute | solution.py:358
  73.4 3.0 %collective-permute-done.6.refs_2_ = bf16[128,256]{1,0:T(8,128)(2,1)S(1)} collective-permute-done((bf16[128,256]{1,0:T(8,128)(2,1)S(1)}, bf16[128,256]{1,0:T(8,128)(2,1)S(1)}, u32[]{:S(2)}, u32[]{:S(2)}) %collective-permute-start.6) | collective-permute-done | bytes 65568 | tf_op jit(solution)/shard_map/grads_back/ppermute | solution.py:358
  76.4 0.0 collective-permute-done.5.refs_1_
  76.4 0.0 copy-done.1
  76.4 0.0 copy-done
  76.4 0.9 input_grad.1
  77.3 17.3 %all_to_all.21 = bf16[32,8,640]{2,1,0:T(8,128)(2,1)S(1)} all-to-all(bf16[32,8,640]{2,1,0:T(8,128)(2,1)S(1)} %bitcast.8), channel_id=1, replica_groups=mesh['x_hi'=2,'z'=8,'core'=2,'x_lo'=2,'y'=4] {'x_hi','z','x_lo'}, dimensions={0} | all-to-all | bytes 655360 | tf_op jit(solution)/shard_map/input_grad/all_to_all | solution.py:394
  94.6 0.7 bitcast_reduce_fusion
Async XLA Ops:
  0.6 26.1 %copy-start.4 = (s32[64]{0:T(128)S(1)}, s32[64]{0:T(128)}, u32[]{:S(2)}) copy-start(s32[64]{0:T(128)} %slot_prompt_ref.3) | copy-start | bytes 772
  0.6 26.1 %copy-start.5 = (s32[16]{0:T(128)S(1)}, s32[16]{0:T(128)}, u32[]{:S(2)}) copy-start(s32[16]{0:T(128)} %owner_ref.3) | copy-start | bytes 196
  4.5 39.6 %copy-start.6 = (bf16[256,1024]{1,0:T(8,128)(2,1)S(1)}, bf16[256,1024]{1,0:T(8,128)(2,1)}, u32[]{:S(2)}) copy-start(bf16[256,1024]{1,0:T(8,128)(2,1)} %q_ref.1) | copy-start | bytes 1572868
  4.5 39.6 %copy-start.7 = (bf16[256,1024]{1,0:T(8,128)(2,1)S(1)}, bf16[256,1024]{1,0:T(8,128)(2,1)}, u32[]{:S(2)}) copy-start(bf16[256,1024]{1,0:T(8,128)(2,1)} %g_ref.1) | copy-start | bytes 1572868
  4.5 39.6 %copy-start.8 = (bf16[256,128]{1,0:T(8,128)(2,1)S(1)}, bf16[256,128]{1,0:T(8,128)(2,1)}, u32[]{:S(2)}) copy-start(bf16[256,128]{1,0:T(8,128)(2,1)} %rk_ref.1) | copy-start | bytes 196612
  4.5 39.6 %copy-start.9 = (bf16[256,128]{1,0:T(8,128)(2,1)S(1)}, bf16[256,128]{1,0:T(8,128)(2,1)}, u32[]{:S(2)}) copy-start(bf16[256,128]{1,0:T(8,128)(2,1)} %rv_ref.1) | copy-start | bytes 196612
  4.5 39.6 %copy-start.10 = (s32[32]{0:T(128)S(1)}, s32[32]{0:T(128)}, u32[]{:S(2)}) copy-start(s32[32]{0:T(128)} %param.21) | copy-start | bytes 388
  4.6 39.6 %copy-start.11 = (s32[16]{0:T(128)S(1)}, s32[16]{0:T(128)}, u32[]{:S(2)}) copy-start(s32[16]{0:T(128)} %param.24) | copy-start | bytes 196
  4.6 20.8 %all-to-all-start = ((bf16[16,32,128]{2,1,0:T(8,128)(2,1)}), bf16[16,32,128]{2,1,0:T(8,128)(2,1)S(1)}, u32[]{:S(2)}, u32[]{:S(2)}) async-start(bf16[16,32,128]{2,1,0:T(8,128)(2,1)} %get-tuple-element.19), calls=%async_computation | async-start | bytes 262144 | tf_op jit(solution)/shard_map/keys_out/all_to_all | solution.py:362
  15.8 19.4 %collective-permute-start.1 = (bf16[2,2,640,128]{3,2,1,0:T(8,128)(2,1)}, bf16[2,2,640,128]{3,2,1,0:T(8,128)(2,1)S(1)}, u32[]{:S(2)}, u32[]{:S(2)}) collective-permute-start(bf16[2,2,640,128]{3,2,1,0:T(8,128)(2,1)} %get-tuple-element.20), channel_id=1, source_target_pairs={{0,1},{1,0},{2,3},{3,2},{4,5},{5,4},{6,7},{7,6},{8,9},{9,8},{10,11... | collective-permute-start | bytes 1966088 | tf_op jit(solution)/shard_map/keys_out/ppermute | solution.py:358
  17.3 17.8 %collective-permute-start.2 = (bf16[2,2,640,128]{3,2,1,0:T(8,128)(2,1)}, bf16[2,2,640,128]{3,2,1,0:T(8,128)(2,1)S(1)}, u32[]{:S(2)}, u32[]{:S(2)}) collective-permute-start(bf16[2,2,640,128]{3,2,1,0:T(8,128)(2,1)} %get-tuple-element.21), channel_id=1, source_target_pairs={{0,3},{1,2},{2,1},{3,0},{4,7},{5,6},{6,5},{7,4},{8,11},{9,10},{10,... | collective-permute-start | bytes 1966088 | tf_op jit(solution)/shard_map/keys_out/ppermute | solution.py:358
  25.4 1.3 %collective-permute-start = (bf16[16,32,128]{2,1,0:T(8,128)(2,1)S(1)}, bf16[16,32,128]{2,1,0:T(8,128)(2,1)S(1)}, u32[]{:S(2)}, u32[]{:S(2)}) collective-permute-start(bf16[16,32,128]{2,1,0:T(8,128)(2,1)S(1)} %all-to-all-done.mine_ref.units_ref), channel_id=1, source_target_pairs={{0,8},{8,0},{1,9},{9,1},{2,10},{10,2},{3,11},{11,3},{4,12},{12,4},... | collective-permute-start | bytes 393224 | tf_op jit(solution)/shard_map/keys_out/ppermute | solution.py:366
  28.0 16.1 %all-to-all-start.1 = ((bf16[16,2,2,16,128]{4,3,2,1,0:T(8,128)(2,1)}), bf16[16,2,2,16,128]{4,3,2,1,0:T(8,128)(2,1)S(1)}, u32[]{:S(2)}, u32[]{:S(2)}) async-start(bf16[16,2,2,16,128]{4,3,2,1,0:T(8,128)(2,1)} %select.1), calls=%async_computation.1 | async-start | bytes 524288 | tf_op jit(solution)/shard_map/keys_out/all_to_all | solution.py:362
  31.9 33.7 %collective-permute-start.3 = (bf16[2,2,640,128]{3,2,1,0:T(8,128)(2,1)}, bf16[2,2,640,128]{3,2,1,0:T(8,128)(2,1)S(1)}, u32[]{:S(2)}, u32[]{:S(2)}) collective-permute-start(bf16[2,2,640,128]{3,2,1,0:T(8,128)(2,1)} %get-tuple-element.29), channel_id=1, source_target_pairs={{0,2},{1,3},{2,0},{3,1},{4,6},{5,7},{6,4},{7,5},{8,10},{9,11},{10,... | collective-permute-start | bytes 1966088 | tf_op jit(solution)/shard_map/keys_out/ppermute | solution.py:358
  44.2 22.8 %copy-start.2 = (f32[2,128,128]{2,1,0:T(8,128)S(1)}, f32[2,128,128]{2,1,0:T(8,128)}, u32[]{:S(2)}) copy-start(f32[2,128,128]{2,1,0:T(8,128)} %constant.4.clone.table_ref) | copy-start | bytes 393220
  44.2 22.7 %copy-start.3 = (f32[128]{0:T(128)S(1)}, f32[128]{0:T(128)}, u32[]{:S(2)}) copy-start(f32[128]{0:T(128)} %param.16) | copy-start | bytes 1540
  44.2 32.2 %copy-start.1 = (bf16[5120,128]{1,0:T(8,128)(2,1)S(1)}, bf16[5120,128]{1,0:T(8,128)(2,1)}, u32[]{:S(2)}) copy-start(bf16[5120,128]{1,0:T(8,128)(2,1)} %wv_ref.3) | copy-start | bytes 3932164
  48.8 27.6 %copy-start = (bf16[5120,128]{1,0:T(8,128)(2,1)S(1)}, bf16[5120,128]{1,0:T(8,128)(2,1)}, u32[]{:S(2)}) copy-start(bf16[5120,128]{1,0:T(8,128)(2,1)} %wk_ref.3) | copy-start | bytes 3932164
  65.6 1.3 %collective-permute-start.4 = (bf16[16,16,128]{2,1,0:T(8,128)(2,1)S(1)}, bf16[16,16,128]{2,1,0:T(8,128)(2,1)S(1)}, u32[]{:S(2)}, u32[]{:S(2)}) collective-permute-start(bf16[16,16,128]{2,1,0:T(8,128)(2,1)S(1)} %get-tuple-element.30), channel_id=1, source_target_pairs={{0,8},{8,0},{1,9},{9,1},{2,10},{10,2},{3,11},{11,3},{4,12},{12,4},... | collective-permute-start | bytes 196616 | tf_op jit(solution)/shard_map/grads_back/ppermute | solution.py:366
  67.2 6.2 %collective-permute-start.7 = (bf16[128,256]{1,0:T(8,128)(2,1)S(1)}, bf16[128,256]{1,0:T(8,128)(2,1)S(1)}, u32[]{:S(2)}, u32[]{:S(2)}) collective-permute-start(bf16[128,256]{1,0:T(8,128)(2,1)S(1)} %unkey.1.refs_0_), channel_id=1, source_target_pairs={{0,3},{1,2},{2,1},{3,0},{4,7},{5,6},{6,5},{7,4},{8,11},{9,10},{10,... | collective-permute-start | bytes 196616 | tf_op jit(solution)/shard_map/grads_back/ppermute | solution.py:358
  70.3 6.1 %collective-permute-start.6 = (bf16[128,256]{1,0:T(8,128)(2,1)S(1)}, bf16[128,256]{1,0:T(8,128)(2,1)S(1)}, u32[]{:S(2)}, u32[]{:S(2)}) collective-permute-start(bf16[128,256]{1,0:T(8,128)(2,1)S(1)} %unkey.1.refs_0_), channel_id=1, source_target_pairs={{0,2},{1,3},{2,0},{3,1},{4,6},{5,7},{6,4},{7,5},{8,10},{9,11},{10,... | collective-permute-start | bytes 196616 | tf_op jit(solution)/shard_map/grads_back/ppermute | solution.py:358
  70.8 5.6 %collective-permute-start.5 = (bf16[128,256]{1,0:T(8,128)(2,1)S(1)}, bf16[128,256]{1,0:T(8,128)(2,1)S(1)}, u32[]{:S(2)}, u32[]{:S(2)}) collective-permute-start(bf16[128,256]{1,0:T(8,128)(2,1)S(1)} %unkey.1.refs_0_), channel_id=1, source_target_pairs={{0,1},{1,0},{2,3},{3,2},{4,5},{5,4},{6,7},{7,6},{8,9},{9,8},{10,11... | collective-permute-start | bytes 196616 | tf_op jit(solution)/shard_map/grads_back/ppermute | solution.py:358

commit v2 on v1

--- a/solution.py
+++ b/solution.py
@@ -16,6 +16,7 @@
 HALF = 128
 CHIPS = 16
 CORES = 2
+PROMPTS = 16
 PIECE = HALF // CHIPS
 UNIT = 2 * PIECE
 WIDTH = 5120
@@ -26,7 +27,7 @@
 EXP2_SCALE = SCALE * float(np.log2(np.e))
 EPS = 1e-06
 FAR = -1e30
-PAIRS = 4
+PAIRS = 2
 f32 = jnp.float32
 bf16 = jnp.bfloat16
 DP = ("x_hi", "z", "core")
@@ -34,7 +35,7 @@
 X_LO = 2
 Y = 4
 PROJECT_VMEM = 60 << 20
-SMEM = pl.BlockSpec(memory_space=pltpu.SMEM)
+LAST_FAR = (1, 3, 2)
 
 
 def rope_table():
@@ -152,11 +153,29 @@
     )(x, wk, wv, gain, table)
 
 
+def owners(slot_prompt_ref, owner_ref):
+    core = lax.axis_index("core")
+    prompts = slot_prompt_ref[...]
+    row = jnp.zeros_like(prompts)
+    for p in range(PROMPTS):
+        row = jnp.where(prompts == p, owner_ref[:, p:p + 1], row)
+    found = []
+    for chip in range(CHIPS):
+        first = chip * CORES * R_CAP
+        found.append(
+            [
+                jnp.where(core == 0, row[0, first + r], row[0, first + R_CAP + r])
+                for r in range(R_CAP)
+            ]
+        )
+    return found
+
+
 def select_kernel(slot_prompt_ref, owner_ref, mine_ref, other_ref, out_ref):
-    core = lax.axis_index("core")
+    found = owners(slot_prompt_ref, owner_ref)
     for chip in range(CHIPS):
         for r in range(R_CAP):
-            q = owner_ref[slot_prompt_ref[chip * CORES * R_CAP + core * R_CAP + r]]
+            q = found[chip][r]
             out_ref[chip, r, 0] = mine_ref[q, :UNIT]
             out_ref[chip, r, 1] = other_ref[q, :UNIT]
 
@@ -165,12 +184,12 @@
     vmem = pl.BlockSpec(memory_space=pltpu.VMEM)
     return pl.pallas_call(
         select_kernel,
-        in_specs=[SMEM, SMEM, vmem, vmem],
+        in_specs=[vmem] * 4,
         out_specs=vmem,
         out_shape=jax.ShapeDtypeStruct((CHIPS, R_CAP, 2, UNIT, HEAD), bf16),
         compiler_params=pltpu.CompilerParams(vmem_limit_bytes=8 << 20),
         name="select",
-    )(slot_prompt, owner, mine, other)
+    )(slot_prompt.reshape(1, -1), owner.reshape(1, -1), mine, other)
 
 
 def attend_slot(core, length, live, kv_ref, q_ref, g_ref, rk_ref, rv_ref, dq_ref, drk_ref, drv_ref, grads_ref, ds_s, pb_s):
@@ -268,11 +287,11 @@
 
 
 def collect_kernel(slot_prompt_ref, owner_ref, got_ref, mine_ref, other_ref, acc):
-    core = lax.axis_index("core")
+    found = owners(slot_prompt_ref, owner_ref)
     acc[...] = jnp.zeros_like(acc)
     for chip in range(CHIPS):
         for r in range(R_CAP):
-            q = owner_ref[slot_prompt_ref[chip * CORES * R_CAP + core * R_CAP + r]]
+            q = found[chip][r]
             acc[q] += got_ref[chip, r].astype(f32)
     mine_ref[...] = acc[:, 0]
     other_ref[...] = acc[:, 1].astype(bf16)
@@ -282,7 +301,7 @@
     vmem = pl.BlockSpec(memory_space=pltpu.VMEM)
     return pl.pallas_call(
         collect_kernel,
-        in_specs=[SMEM, SMEM, vmem],
+        in_specs=[vmem] * 3,
         out_specs=[vmem, vmem],
         out_shape=[
             jax.ShapeDtypeStruct((CHIPS, UNIT, HEAD), f32),
@@ -291,7 +310,7 @@
         scratch_shapes=[pltpu.VMEM((CHIPS, 2, UNIT, HEAD), f32)],
         compiler_params=pltpu.CompilerParams(vmem_limit_bytes=8 << 20),
         name="collect",
-    )(slot_prompt, owner, got)
+    )(slot_prompt.reshape(1, -1), owner.reshape(1, -1), got)
 
 
 def unkey_kernel(sum_ref, other_ref, units_ref, gain_ref, table_ref, out_ref):
@@ -332,7 +351,7 @@
         total = dot_nt(grads[0][...], jnp.concatenate([wk_ref[rows], wv_ref[rows]], axis=1))
         for k in range(1, Y):
             w = jnp.concatenate([got[k - 1][half, 0], got[k - 1][half, 1]], axis=1)
-            total += dot_nt(grads[k][...], w)
+            total += dot_nt(grads[1 + LAST_FAR.index(k)][...], w)
         out_ref[:, half] = total.reshape(CHIPS, PIECE, COLS).astype(bf16)
 
 
@@ -387,7 +406,7 @@
         sums, other = collect(slot_prompt, prompt_owner, spread(grads))
         other, got[1] = together(other, got[1])
         both = unkey(sums, swap_cores(other), mine, gain, table)
-        both = [both] + [swap_y(both, k) for k in range(1, Y)]
+        both = [both] + [swap_y(both, k) for k in LAST_FAR]
     with jax.named_scope("input_grad"):
         shares = input_grad(key_matrix, value_matrix, both, got)
         shares = shares.reshape(CHIPS * X_LO, PIECE, COLS)

time: 95.9 us -> 95.4 us (level)
  transfers between devices with their start and end apart: 10 -> 10, of which waited for: 6 -> 6; matrix products, arithmetic and copies ran while one was open for 0% -> 0% of each run, Pallas kernels for 7% -> 6%
where the time goes in v2:
time: 95.4 us; the launch traced here: 94 us
  blocking collectives  33.7 us (35%)
  starting transfers between devices  26.3 us (28%)
  waiting for transfers between devices  21.9 us (23%)
  Pallas kernels  10.6 us (11%)
    all_to_all x1, blocking collectives, on_device(): shares = lax.all_to_all(shares, SPREAD + ('x_lo',), 0, 0, tiled=True)  17.6 us
    all_to_all x1, blocking collectives, spread(): return lax.all_to_all(x, SPREAD, 0, 0, tiled=True)  16.1 us
    all_to_all x2, starting transfers between devices, spread(): return lax.all_to_all(x, SPREAD, 0, 0, tiled=True)  15.1 us
    all_to_all x2, waiting for transfers between devices, spread(): return lax.all_to_all(x, SPREAD, 0, 0, tiled=True)  14.9 us
    ppermute x6, starting transfers between devices, swap_y(): return lax.ppermute(x, 'y', [(i, i ^ k) for i in range(Y)])  11.1 us
    ppermute x6, waiting for transfers between devices, swap_y(): return lax.ppermute(x, 'y', [(i, i ^ k) for i in range(Y)])  4.43 us
    pallas_call x1, Pallas kernels, attend(): pl.pallas_call(attend_kernel, in_specs=[vmem] * 8, out_specs=[vmem] * 4,...  4.3 us
    pallas_call x1, Pallas kernels, project(): pl.pallas_call(project_kernel, in_specs=[hbm] * 5, out_specs=[vmem] + [an...  3.84 us
  transfers between devices with their start and end apart: 10, of which 6 were waited for; matrix products, arithmetic and copies ran while one was open for 0% of the time, Pallas kernels for 6%

profile of v2, /device:TPU:32, one launch (start us, length us, event | category | flops | bytes accessed | tf_op | source)
XLA Modules:
  0.0 94.0 jit_solution(9645905757880939975)
XLA Ops:
  0.6 0.0 copy-start.4
  0.6 0.0 copy-start.5
  0.7 3.8 %project.1 = (bf16[16,32,128]{2,1,0:T(8,128)(2,1)}, bf16[2,2,640,128]{3,2,1,0:T(8,128)(2,1)}, bf16[2,2,640,128]{3,2,1,0:T(8,128)(2,1)}, bf16[2,2,640,128]{3,2,1,0:T(8,128)(2,1)}) custom-call(bf16[128,5120]{1,0:T(8,128)(2,1)} %x_ref.1, bf16[5120,128]{1,0:T(8,128)(2,1)} %wk_ref.3, bf16[5120,128]{1,0:T(8,128)(2,1)} %wv_ref.3, f32[1,128]{1,0:T(1,128)} %bitcast.10, ...), custom_call_target="tpu_custom_call" | custom-call | flops 335544320 | bytes 4194304 | tf_op jit(solution)/shard_map/keys_out/project/pallas_call | solution.py:135
  4.5 0.0 copy-start.6
  4.5 0.0 copy-start.7
  4.5 0.0 copy-start.8
  4.5 0.0 copy-start.9
  4.5 0.0 copy-start.10
  4.6 0.0 copy-start.11
  4.6 11.2 %all-to-all-start = ((bf16[16,32,128]{2,1,0:T(8,128)(2,1)}), bf16[16,32,128]{2,1,0:T(8,128)(2,1)S(1)}, u32[]{:S(2)}, u32[]{:S(2)}) async-start(bf16[16,32,128]{2,1,0:T(8,128)(2,1)} %get-tuple-element.19), calls=%async_computation | async-start | bytes 262144 | tf_op jit(solution)/shard_map/keys_out/all_to_all | solution.py:381
  15.8 1.6 %collective-permute-start.1 = (bf16[2,2,640,128]{3,2,1,0:T(8,128)(2,1)}, bf16[2,2,640,128]{3,2,1,0:T(8,128)(2,1)S(1)}, u32[]{:S(2)}, u32[]{:S(2)}) collective-permute-start(bf16[2,2,640,128]{3,2,1,0:T(8,128)(2,1)} %get-tuple-element.20), channel_id=1, source_target_pairs={{0,1},{1,0},{2,3},{3,2},{4,5},{5,4},{6,7},{7,6},{8,9},{9,8},{10,11... | collective-permute-start | bytes 1966088 | tf_op jit(solution)/shard_map/keys_out/ppermute | solution.py:377
  17.3 2.2 %collective-permute-start.2 = (bf16[2,2,640,128]{3,2,1,0:T(8,128)(2,1)}, bf16[2,2,640,128]{3,2,1,0:T(8,128)(2,1)S(1)}, u32[]{:S(2)}, u32[]{:S(2)}) collective-permute-start(bf16[2,2,640,128]{3,2,1,0:T(8,128)(2,1)} %get-tuple-element.21), channel_id=1, source_target_pairs={{0,3},{1,2},{2,1},{3,0},{4,7},{5,6},{6,5},{7,4},{8,11},{9,10},{10,... | collective-permute-start | bytes 1966088 | tf_op jit(solution)/shard_map/keys_out/ppermute | solution.py:377
  19.5 5.8 %all-to-all-done.mine_ref.units_ref = bf16[16,32,128]{2,1,0:T(8,128)(2,1)S(1)} async-done(((bf16[16,32,128]{2,1,0:T(8,128)(2,1)}), bf16[16,32,128]{2,1,0:T(8,128)(2,1)S(1)}, u32[]{:S(2)}, u32[]{:S(2)}) %all-to-all-start) | async-done | bytes 131104 | tf_op jit(solution)/shard_map/keys_out/all_to_all | solution.py:381
  25.4 0.0 collective-permute-start
  25.4 1.3 %collective-permute-done.other_ref = bf16[16,32,128]{2,1,0:T(8,128)(2,1)S(1)} collective-permute-done((bf16[16,32,128]{2,1,0:T(8,128)(2,1)S(1)}, bf16[16,32,128]{2,1,0:T(8,128)(2,1)S(1)}, u32[]{:S(2)}, u32[]{:S(2)}) %collective-permute-start) | collective-permute-done | bytes 131104 | tf_op jit(solution)/shard_map/keys_out/ppermute | solution.py:385
  26.7 0.0 copy-done.4
  26.7 0.0 copy-done.5
  26.7 1.0 %select.1 = bf16[16,2,2,16,128]{4,3,2,1,0:T(8,128)(2,1)} custom-call(s32[1,64]{1,0:T(1,128)S(1)} %bitcast.12, s32[1,16]{1,0:T(1,128)S(1)} %bitcast.15, bf16[16,32,128]{2,1,0:T(8,128)(2,1)S(1)} %all-to-all-done.mine_ref.units_ref, bf16[16,32,128]{2,1,0:T(8,128)(2,1)S(1)} %collective-permute-done.other_ref), custom_call_target="tpu_custom_call" | custom-call | tf_op jit(solution)/shard_map/keys_out/select/pallas_call | solution.py:185
  27.7 3.9 %all-to-all-start.1 = ((bf16[16,2,2,16,128]{4,3,2,1,0:T(8,128)(2,1)}), bf16[16,2,2,16,128]{4,3,2,1,0:T(8,128)(2,1)S(1)}, u32[]{:S(2)}, u32[]{:S(2)}) async-start(bf16[16,2,2,16,128]{4,3,2,1,0:T(8,128)(2,1)} %select.1), calls=%async_computation.1 | async-start | bytes 524288 | tf_op jit(solution)/shard_map/keys_out/all_to_all | solution.py:381
  31.6 3.2 %collective-permute-start.3 = (bf16[2,2,640,128]{3,2,1,0:T(8,128)(2,1)}, bf16[2,2,640,128]{3,2,1,0:T(8,128)(2,1)S(1)}, u32[]{:S(2)}, u32[]{:S(2)}) collective-permute-start(bf16[2,2,640,128]{3,2,1,0:T(8,128)(2,1)} %get-tuple-element.29), channel_id=1, source_target_pairs={{0,2},{1,3},{2,0},{3,1},{4,6},{5,7},{6,4},{7,5},{8,10},{9,11},{10,... | collective-permute-start | bytes 1966088 | tf_op jit(solution)/shard_map/keys_out/ppermute | solution.py:377
  34.8 0.0 collective-permute-done.1.refs_4_
  34.8 0.0 collective-permute-done.2.refs_6_
  34.8 9.0 %all-to-all-done.1.kv_ref = bf16[16,2,2,16,128]{4,3,2,1,0:T(8,128)(2,1)S(1)} async-done(((bf16[16,2,2,16,128]{4,3,2,1,0:T(8,128)(2,1)}), bf16[16,2,2,16,128]{4,3,2,1,0:T(8,128)(2,1)S(1)}, u32[]{:S(2)}, u32[]{:S(2)}) %all-to-all-start.1) | async-done | bytes 262176 | tf_op jit(solution)/shard_map/keys_out/all_to_all | solution.py:381
  43.8 0.0 copy-done.6
  43.8 0.0 copy-done.7
  43.8 0.0 copy-done.8
  43.8 0.0 copy-done.9
  43.8 0.0 copy-done.10
  43.8 0.0 copy-done.11
  43.9 0.0 copy-start.2
  43.9 0.0 copy-start.3
  43.9 0.0 copy-start.1
  43.9 4.3 %attend.1 = (bf16[256,1024]{1,0:T(8,128)(2,1)}, bf16[256,128]{1,0:T(8,128)(2,1)}, bf16[256,128]{1,0:T(8,128)(2,1)}, bf16[16,2,2,16,128]{4,3,2,1,0:T(8,128)(2,1)S(1)}) custom-call(s32[1,32]{1,0:T(1,128)S(1)} %bitcast.17, s32[1,64]{1,0:T(1,128)S(1)} %bitcast.13, s32[1,16]{1,0:T(1,128)S(1)} %bitcast.18, bf16[16,2,2,16,128]{4,3,2,1,0:T(8,128)(2,1)S(1)} %all-to-all-done.1.kv_ref, ...), custom_call_target="tpu_custom_call" | custom-call | flops 1006632960 | bytes 3145728 | tf_op jit(solution)/shard_map/attention/attend/pallas_call | solution.py:269
  48.2 0.0 copy-start
  48.2 16.1 %all_to_all.20.got_ref = bf16[16,2,2,16,128]{4,3,2,1,0:T(8,128)(2,1)S(1)} all-to-all(bf16[16,2,2,16,128]{4,3,2,1,0:T(8,128)(2,1)S(1)} %get-tuple-element.26), channel_id=1, replica_groups=mesh['x_hi'=2,'z'=8,'core'=2,'x_lo'=2,'y'=4] {'x_hi','z'}, dimensions={0} | all-to-all | bytes 524288 | tf_op jit(solution)/shard_map/grads_back/all_to_all | solution.py:381
  64.3 0.3 collect.1
  64.6 0.0 collective-permute-done.3.refs_5_
  64.7 0.1 collective-permute-start.4
  64.8 1.2 %collective-permute-done.4.other_ref = bf16[16,16,128]{2,1,0:T(8,128)(2,1)S(1)} collective-permute-done((bf16[16,16,128]{2,1,0:T(8,128)(2,1)S(1)}, bf16[16,16,128]{2,1,0:T(8,128)(2,1)S(1)}, u32[]{:S(2)}, u32[]{:S(2)}) %collective-permute-start.4) | collective-permute-done | bytes 65568 | tf_op jit(solution)/shard_map/grads_back/ppermute | solution.py:385
  66.0 0.0 copy-done.2
  66.0 0.0 copy-done.3
  66.0 0.2 unkey.1.refs_0_
  66.3 3.1 %collective-permute-start.7 = (bf16[128,256]{1,0:T(8,128)(2,1)S(1)}, bf16[128,256]{1,0:T(8,128)(2,1)S(1)}, u32[]{:S(2)}, u32[]{:S(2)}) collective-permute-start(bf16[128,256]{1,0:T(8,128)(2,1)S(1)} %unkey.1.refs_0_), channel_id=1, source_target_pairs={{0,2},{1,3},{2,0},{3,1},{4,6},{5,7},{6,4},{7,5},{8,10},{9,11},{10,... | collective-permute-start | bytes 196616 | tf_op jit(solution)/shard_map/grads_back/ppermute | solution.py:377
  69.4 1.1 %collective-permute-start.6 = (bf16[128,256]{1,0:T(8,128)(2,1)S(1)}, bf16[128,256]{1,0:T(8,128)(2,1)S(1)}, u32[]{:S(2)}, u32[]{:S(2)}) collective-permute-start(bf16[128,256]{1,0:T(8,128)(2,1)S(1)} %unkey.1.refs_0_), channel_id=1, source_target_pairs={{0,3},{1,2},{2,1},{3,0},{4,7},{5,6},{6,5},{7,4},{8,11},{9,10},{10,... | collective-permute-start | bytes 196616 | tf_op jit(solution)/shard_map/grads_back/ppermute | solution.py:377
  70.5 0.0 collective-permute-start.5
  70.5 1.7 %collective-permute-done.7.refs_3_ = bf16[128,256]{1,0:T(8,128)(2,1)S(1)} collective-permute-done((bf16[128,256]{1,0:T(8,128)(2,1)S(1)}, bf16[128,256]{1,0:T(8,128)(2,1)S(1)}, u32[]{:S(2)}, u32[]{:S(2)}) %collective-permute-start.7) | collective-permute-done | bytes 65568 | tf_op jit(solution)/shard_map/grads_back/ppermute | solution.py:377
  72.1 2.8 %collective-permute-done.6.refs_2_ = bf16[128,256]{1,0:T(8,128)(2,1)S(1)} collective-permute-done((bf16[128,256]{1,0:T(8,128)(2,1)S(1)}, bf16[128,256]{1,0:T(8,128)(2,1)S(1)}, u32[]{:S(2)}, u32[]{:S(2)}) %collective-permute-start.6) | collective-permute-done | bytes 65568 | tf_op jit(solution)/shard_map/grads_back/ppermute | solution.py:377
  74.9 0.0 collective-permute-done.5.refs_1_
  74.9 0.0 copy-done.1
  74.9 0.0 copy-done
  74.9 0.9 input_grad.1
  75.8 17.6 %all_to_all.21 = bf16[32,8,640]{2,1,0:T(8,128)(2,1)S(1)} all-to-all(bf16[32,8,640]{2,1,0:T(8,128)(2,1)S(1)} %bitcast.9), channel_id=1, replica_groups=mesh['x_hi'=2,'z'=8,'core'=2,'x_lo'=2,'y'=4] {'x_hi','z','x_lo'}, dimensions={0} | all-to-all | bytes 655360 | tf_op jit(solution)/shard_map/input_grad/all_to_all | solution.py:413
  93.3 0.7 bitcast_reduce_fusion
Async XLA Ops:
  0.6 26.1 %copy-start.4 = (s32[64]{0:T(128)S(1)}, s32[64]{0:T(128)}, u32[]{:S(2)}) copy-start(s32[64]{0:T(128)} %param.22) | copy-start | bytes 772
  0.6 26.1 %copy-start.5 = (s32[16]{0:T(128)S(1)}, s32[16]{0:T(128)}, u32[]{:S(2)}) copy-start(s32[16]{0:T(128)} %param.23) | copy-start | bytes 196
  4.5 39.3 %copy-start.6 = (bf16[256,1024]{1,0:T(8,128)(2,1)S(1)}, bf16[256,1024]{1,0:T(8,128)(2,1)}, u32[]{:S(2)}) copy-start(bf16[256,1024]{1,0:T(8,128)(2,1)} %q_ref.1) | copy-start | bytes 1572868
  4.5 39.3 %copy-start.7 = (bf16[256,1024]{1,0:T(8,128)(2,1)S(1)}, bf16[256,1024]{1,0:T(8,128)(2,1)}, u32[]{:S(2)}) copy-start(bf16[256,1024]{1,0:T(8,128)(2,1)} %g_ref.1) | copy-start | bytes 1572868
  4.5 39.3 %copy-start.8 = (bf16[256,128]{1,0:T(8,128)(2,1)S(1)}, bf16[256,128]{1,0:T(8,128)(2,1)}, u32[]{:S(2)}) copy-start(bf16[256,128]{1,0:T(8,128)(2,1)} %rk_ref.1) | copy-start | bytes 196612
  4.5 39.3 %copy-start.9 = (bf16[256,128]{1,0:T(8,128)(2,1)S(1)}, bf16[256,128]{1,0:T(8,128)(2,1)}, u32[]{:S(2)}) copy-start(bf16[256,128]{1,0:T(8,128)(2,1)} %rv_ref.1) | copy-start | bytes 196612
  4.5 39.3 %copy-start.10 = (s32[32]{0:T(128)S(1)}, s32[32]{0:T(128)}, u32[]{:S(2)}) copy-start(s32[32]{0:T(128)} %param.21) | copy-start | bytes 388
  4.6 39.3 %copy-start.11 = (s32[16]{0:T(128)S(1)}, s32[16]{0:T(128)}, u32[]{:S(2)}) copy-start(s32[16]{0:T(128)} %param.24) | copy-start | bytes 196
  4.6 20.8 %all-to-all-start = ((bf16[16,32,128]{2,1,0:T(8,128)(2,1)}), bf16[16,32,128]{2,1,0:T(8,128)(2,1)S(1)}, u32[]{:S(2)}, u32[]{:S(2)}) async-start(bf16[16,32,128]{2,1,0:T(8,128)(2,1)} %get-tuple-element.19), calls=%async_computation | async-start | bytes 262144 | tf_op jit(solution)/shard_map/keys_out/all_to_all | solution.py:381
  15.8 19.0 %collective-permute-start.1 = (bf16[2,2,640,128]{3,2,1,0:T(8,128)(2,1)}, bf16[2,2,640,128]{3,2,1,0:T(8,128)(2,1)S(1)}, u32[]{:S(2)}, u32[]{:S(2)}) collective-permute-start(bf16[2,2,640,128]{3,2,1,0:T(8,128)(2,1)} %get-tuple-element.20), channel_id=1, source_target_pairs={{0,1},{1,0},{2,3},{3,2},{4,5},{5,4},{6,7},{7,6},{8,9},{9,8},{10,11... | collective-permute-start | bytes 1966088 | tf_op jit(solution)/shard_map/keys_out/ppermute | solution.py:377
  17.3 17.5 %collective-permute-start.2 = (bf16[2,2,640,128]{3,2,1,0:T(8,128)(2,1)}, bf16[2,2,640,128]{3,2,1,0:T(8,128)(2,1)S(1)}, u32[]{:S(2)}, u32[]{:S(2)}) collective-permute-start(bf16[2,2,640,128]{3,2,1,0:T(8,128)(2,1)} %get-tuple-element.21), channel_id=1, source_target_pairs={{0,3},{1,2},{2,1},{3,0},{4,7},{5,6},{6,5},{7,4},{8,11},{9,10},{10,... | collective-permute-start | bytes 1966088 | tf_op jit(solution)/shard_map/keys_out/ppermute | solution.py:377
  25.4 1.3 %collective-permute-start = (bf16[16,32,128]{2,1,0:T(8,128)(2,1)S(1)}, bf16[16,32,128]{2,1,0:T(8,128)(2,1)S(1)}, u32[]{:S(2)}, u32[]{:S(2)}) collective-permute-start(bf16[16,32,128]{2,1,0:T(8,128)(2,1)S(1)} %all-to-all-done.mine_ref.units_ref), channel_id=1, source_target_pairs={{0,8},{8,0},{1,9},{9,1},{2,10},{10,2},{3,11},{11,3},{4,12},{12,4},... | collective-permute-start | bytes 393224 | tf_op jit(solution)/shard_map/keys_out/ppermute | solution.py:385
  27.7 16.1 %all-to-all-start.1 = ((bf16[16,2,2,16,128]{4,3,2,1,0:T(8,128)(2,1)}), bf16[16,2,2,16,128]{4,3,2,1,0:T(8,128)(2,1)S(1)}, u32[]{:S(2)}, u32[]{:S(2)}) async-start(bf16[16,2,2,16,128]{4,3,2,1,0:T(8,128)(2,1)} %select.1), calls=%async_computation.1 | async-start | bytes 524288 | tf_op jit(solution)/shard_map/keys_out/all_to_all | solution.py:381
  31.6 33.1 %collective-permute-start.3 = (bf16[2,2,640,128]{3,2,1,0:T(8,128)(2,1)}, bf16[2,2,640,128]{3,2,1,0:T(8,128)(2,1)S(1)}, u32[]{:S(2)}, u32[]{:S(2)}) collective-permute-start(bf16[2,2,640,128]{3,2,1,0:T(8,128)(2,1)} %get-tuple-element.29), channel_id=1, source_target_pairs={{0,2},{1,3},{2,0},{3,1},{4,6},{5,7},{6,4},{7,5},{8,10},{9,11},{10,... | collective-permute-start | bytes 1966088 | tf_op jit(solution)/shard_map/keys_out/ppermute | solution.py:377
  43.9 22.2 %copy-start.2 = (f32[2,128,128]{2,1,0:T(8,128)S(1)}, f32[2,128,128]{2,1,0:T(8,128)}, u32[]{:S(2)}) copy-start(f32[2,128,128]{2,1,0:T(8,128)} %constant.4.clone.table_ref) | copy-start | bytes 393220
  43.9 22.1 %copy-start.3 = (f32[128]{0:T(128)S(1)}, f32[128]{0:T(128)}, u32[]{:S(2)}) copy-start(f32[128]{0:T(128)} %param.16) | copy-start | bytes 1540
  43.9 31.0 %copy-start.1 = (bf16[5120,128]{1,0:T(8,128)(2,1)S(1)}, bf16[5120,128]{1,0:T(8,128)(2,1)}, u32[]{:S(2)}) copy-start(bf16[5120,128]{1,0:T(8,128)(2,1)} %wv_ref.3) | copy-start | bytes 3932164
  48.2 26.7 %copy-start = (bf16[5120,128]{1,0:T(8,128)(2,1)S(1)}, bf16[5120,128]{1,0:T(8,128)(2,1)}, u32[]{:S(2)}) copy-start(bf16[5120,128]{1,0:T(8,128)(2,1)} %wk_ref.3) | copy-start | bytes 3932164
  64.7 1.3 %collective-permute-start.4 = (bf16[16,16,128]{2,1,0:T(8,128)(2,1)S(1)}, bf16[16,16,128]{2,1,0:T(8,128)(2,1)S(1)}, u32[]{:S(2)}, u32[]{:S(2)}) collective-permute-start(bf16[16,16,128]{2,1,0:T(8,128)(2,1)S(1)} %get-tuple-element.30), channel_id=1, source_target_pairs={{0,8},{8,0},{1,9},{9,1},{2,10},{10,2},{3,11},{11,3},{4,12},{12,4},... | collective-permute-start | bytes 196616 | tf_op jit(solution)/shard_map/grads_back/ppermute | solution.py:385
  66.3 5.9 %collective-permute-start.7 = (bf16[128,256]{1,0:T(8,128)(2,1)S(1)}, bf16[128,256]{1,0:T(8,128)(2,1)S(1)}, u32[]{:S(2)}, u32[]{:S(2)}) collective-permute-start(bf16[128,256]{1,0:T(8,128)(2,1)S(1)} %unkey.1.refs_0_), channel_id=1, source_target_pairs={{0,2},{1,3},{2,0},{3,1},{4,6},{5,7},{6,4},{7,5},{8,10},{9,11},{10,... | collective-permute-start | bytes 196616 | tf_op jit(solution)/shard_map/grads_back/ppermute | solution.py:377
  69.4 5.5 %collective-permute-start.6 = (bf16[128,256]{1,0:T(8,128)(2,1)S(1)}, bf16[128,256]{1,0:T(8,128)(2,1)S(1)}, u32[]{:S(2)}, u32[]{:S(2)}) collective-permute-start(bf16[128,256]{1,0:T(8,128)(2,1)S(1)} %unkey.1.refs_0_), channel_id=1, source_target_pairs={{0,3},{1,2},{2,1},{3,0},{4,7},{5,6},{6,5},{7,4},{8,11},{9,10},{10,... | collective-permute-start | bytes 196616 | tf_op jit(solution)/shard_map/grads_back/ppermute | solution.py:377
  70.5 4.4 %collective-permute-start.5 = (bf16[128,256]{1,0:T(8,128)(2,1)S(1)}, bf16[128,256]{1,0:T(8,128)(2,1)S(1)}, u32[]{:S(2)}, u32[]{:S(2)}) collective-permute-start(bf16[128,256]{1,0:T(8,128)(2,1)S(1)} %unkey.1.refs_0_), channel_id=1, source_target_pairs={{0,1},{1,0},{2,3},{3,2},{4,5},{5,4},{6,7},{7,6},{8,9},{9,8},{10,11... | collective-permute-start | bytes 196616 | tf_op jit(solution)/shard_map/grads_back/ppermute | solution.py:377

commit v3 on v2

--- a/solution.py
+++ b/solution.py
@@ -352,7 +352,7 @@
         for k in range(1, Y):
             w = jnp.concatenate([got[k - 1][half, 0], got[k - 1][half, 1]], axis=1)
             total += dot_nt(grads[1 + LAST_FAR.index(k)][...], w)
-        out_ref[:, half] = total.reshape(CHIPS, PIECE, COLS).astype(bf16)
+        out_ref[half] = total.reshape(CHIPS, PIECE, COLS).astype(bf16)
 
 
 def input_grad(wk, wv, grads, got):
@@ -361,7 +361,7 @@
         input_grad_kernel,
         in_specs=[vmem] * (2 * Y + 1),
         out_specs=vmem,
-        out_shape=jax.ShapeDtypeStruct((CHIPS, X_LO, PIECE, COLS), bf16),
+        out_shape=jax.ShapeDtypeStruct((X_LO, CHIPS, PIECE, COLS), bf16),
         compiler_params=pltpu.CompilerParams(vmem_limit_bytes=16 << 20),
         cost_estimate=pl.CostEstimate(flops=2 * HALF * WIDTH * 256, bytes_accessed=4 << 20, transcendentals=0),
         name="input_grad",
@@ -409,10 +409,10 @@
         both = [both] + [swap_y(both, k) for k in LAST_FAR]
     with jax.named_scope("input_grad"):
         shares = input_grad(key_matrix, value_matrix, both, got)
-        shares = shares.reshape(CHIPS * X_LO, PIECE, COLS)
-        shares = lax.all_to_all(shares, SPREAD + ("x_lo",), 0, 0, tiled=True)
-        shares = shares.reshape(CHIPS, X_LO, PIECE, COLS).astype(f32)
-        d_prompt = jnp.sum(shares, axis=1).reshape(HALF, COLS).astype(bf16)
+        shares = shares.reshape(X_LO * CHIPS, PIECE, COLS)
+        shares = lax.all_to_all(shares, ("x_lo",) + SPREAD, 0, 0, tiled=True)
+        shares = shares.reshape(X_LO, CHIPS, PIECE, COLS).astype(f32)
+        d_prompt = jnp.sum(shares, axis=0).reshape(HALF, COLS).astype(bf16)
     return dq, drk, drv, d_prompt
 
 

time: 95.4 us -> 94.1 us (0.986); the launches traced: 94 us -> 93.7 us
  no operation moved by 1% of the time
where the time goes in v3:
time: 94.1 us; the launch traced here: 93.7 us
  blocking collectives  33.3 us (35%)
  starting transfers between devices  26.3 us (28%)
  waiting for transfers between devices  21.9 us (23%)
  Pallas kernels  10.6 us (11%)
    all_to_all x1, blocking collectives, on_device(): shares = lax.all_to_all(shares, ('x_lo',) + SPREAD, 0, 0, tiled=True)  17.2 us
    all_to_all x1, blocking collectives, spread(): return lax.all_to_all(x, SPREAD, 0, 0, tiled=True)  16.1 us
    all_to_all x2, starting transfers between devices, spread(): return lax.all_to_all(x, SPREAD, 0, 0, tiled=True)  15.1 us
    all_to_all x2, waiting for transfers between devices, spread(): return lax.all_to_all(x, SPREAD, 0, 0, tiled=True)  14.9 us
    ppermute x6, starting transfers between devices, swap_y(): return lax.ppermute(x, 'y', [(i, i ^ k) for i in range(Y)])  11.1 us
    ppermute x6, waiting for transfers between devices, swap_y(): return lax.ppermute(x, 'y', [(i, i ^ k) for i in range(Y)])  4.43 us
    pallas_call x1, Pallas kernels, attend(): pl.pallas_call(attend_kernel, in_specs=[vmem] * 8, out_specs=[vmem] * 4,...  4.3 us
    pallas_call x1, Pallas kernels, project(): pl.pallas_call(project_kernel, in_specs=[hbm] * 5, out_specs=[vmem] + [an...  3.84 us
  transfers between devices with their start and end apart: 10, of which 6 were waited for; matrix products, arithmetic and copies ran while one was open for 0% of the time, Pallas kernels for 6%

profile of v3, /device:TPU:32, one launch (start us, length us, event | category | flops | bytes accessed | tf_op | source)
XLA Modules:
  0.0 93.7 jit_solution(15322680531642030540)
XLA Ops:
  0.6 0.0 copy-start.4
  0.6 0.0 copy-start.5
  0.7 3.8 %project.1 = (bf16[16,32,128]{2,1,0:T(8,128)(2,1)}, bf16[2,2,640,128]{3,2,1,0:T(8,128)(2,1)}, bf16[2,2,640,128]{3,2,1,0:T(8,128)(2,1)}, bf16[2,2,640,128]{3,2,1,0:T(8,128)(2,1)}) custom-call(bf16[128,5120]{1,0:T(8,128)(2,1)} %x_ref.1, bf16[5120,128]{1,0:T(8,128)(2,1)} %wk_ref.3, bf16[5120,128]{1,0:T(8,128)(2,1)} %wv_ref.3, f32[1,128]{1,0:T(1,128)} %bitcast.9, ...), custom_call_target="tpu_custom_call" | custom-call | flops 335544320 | bytes 4194304 | tf_op jit(solution)/shard_map/keys_out/project/pallas_call | solution.py:135
  4.5 0.0 copy-start.6
  4.5 0.0 copy-start.7
  4.5 0.0 copy-start.8
  4.5 0.0 copy-start.9
  4.5 0.0 copy-start.10
  4.6 0.0 copy-start.11
  4.6 11.2 %all-to-all-start = ((bf16[16,32,128]{2,1,0:T(8,128)(2,1)}), bf16[16,32,128]{2,1,0:T(8,128)(2,1)S(1)}, u32[]{:S(2)}, u32[]{:S(2)}) async-start(bf16[16,32,128]{2,1,0:T(8,128)(2,1)} %get-tuple-element.19), calls=%async_computation | async-start | bytes 262144 | tf_op jit(solution)/shard_map/keys_out/all_to_all | solution.py:381
  15.8 1.6 %collective-permute-start.1 = (bf16[2,2,640,128]{3,2,1,0:T(8,128)(2,1)}, bf16[2,2,640,128]{3,2,1,0:T(8,128)(2,1)S(1)}, u32[]{:S(2)}, u32[]{:S(2)}) collective-permute-start(bf16[2,2,640,128]{3,2,1,0:T(8,128)(2,1)} %get-tuple-element.20), channel_id=1, source_target_pairs={{0,1},{1,0},{2,3},{3,2},{4,5},{5,4},{6,7},{7,6},{8,9},{9,8},{10,11... | collective-permute-start | bytes 1966088 | tf_op jit(solution)/shard_map/keys_out/ppermute | solution.py:377
  17.3 2.2 %collective-permute-start.2 = (bf16[2,2,640,128]{3,2,1,0:T(8,128)(2,1)}, bf16[2,2,640,128]{3,2,1,0:T(8,128)(2,1)S(1)}, u32[]{:S(2)}, u32[]{:S(2)}) collective-permute-start(bf16[2,2,640,128]{3,2,1,0:T(8,128)(2,1)} %get-tuple-element.21), channel_id=1, source_target_pairs={{0,3},{1,2},{2,1},{3,0},{4,7},{5,6},{6,5},{7,4},{8,11},{9,10},{10,... | collective-permute-start | bytes 1966088 | tf_op jit(solution)/shard_map/keys_out/ppermute | solution.py:377
  19.5 5.8 %all-to-all-done.mine_ref.units_ref = bf16[16,32,128]{2,1,0:T(8,128)(2,1)S(1)} async-done(((bf16[16,32,128]{2,1,0:T(8,128)(2,1)}), bf16[16,32,128]{2,1,0:T(8,128)(2,1)S(1)}, u32[]{:S(2)}, u32[]{:S(2)}) %all-to-all-start) | async-done | bytes 131104 | tf_op jit(solution)/shard_map/keys_out/all_to_all | solution.py:381
  25.4 0.0 collective-permute-start
  25.4 1.3 %collective-permute-done.other_ref = bf16[16,32,128]{2,1,0:T(8,128)(2,1)S(1)} collective-permute-done((bf16[16,32,128]{2,1,0:T(8,128)(2,1)S(1)}, bf16[16,32,128]{2,1,0:T(8,128)(2,1)S(1)}, u32[]{:S(2)}, u32[]{:S(2)}) %collective-permute-start) | collective-permute-done | bytes 131104 | tf_op jit(solution)/shard_map/keys_out/ppermute | solution.py:385
  26.7 0.0 copy-done.4
  26.7 0.0 copy-done.5
  26.7 1.0 %select.1 = bf16[16,2,2,16,128]{4,3,2,1,0:T(8,128)(2,1)} custom-call(s32[1,64]{1,0:T(1,128)S(1)} %bitcast.11, s32[1,16]{1,0:T(1,128)S(1)} %bitcast.14, bf16[16,32,128]{2,1,0:T(8,128)(2,1)S(1)} %all-to-all-done.mine_ref.units_ref, bf16[16,32,128]{2,1,0:T(8,128)(2,1)S(1)} %collective-permute-done.other_ref), custom_call_target="tpu_custom_call" | custom-call | tf_op jit(solution)/shard_map/keys_out/select/pallas_call | solution.py:185
  27.7 3.9 %all-to-all-start.1 = ((bf16[16,2,2,16,128]{4,3,2,1,0:T(8,128)(2,1)}), bf16[16,2,2,16,128]{4,3,2,1,0:T(8,128)(2,1)S(1)}, u32[]{:S(2)}, u32[]{:S(2)}) async-start(bf16[16,2,2,16,128]{4,3,2,1,0:T(8,128)(2,1)} %select.1), calls=%async_computation.1 | async-start | bytes 524288 | tf_op jit(solution)/shard_map/keys_out/all_to_all | solution.py:381
  31.6 3.2 %collective-permute-start.3 = (bf16[2,2,640,128]{3,2,1,0:T(8,128)(2,1)}, bf16[2,2,640,128]{3,2,1,0:T(8,128)(2,1)S(1)}, u32[]{:S(2)}, u32[]{:S(2)}) collective-permute-start(bf16[2,2,640,128]{3,2,1,0:T(8,128)(2,1)} %get-tuple-element.29), channel_id=1, source_target_pairs={{0,2},{1,3},{2,0},{3,1},{4,6},{5,7},{6,4},{7,5},{8,10},{9,11},{10,... | collective-permute-start | bytes 1966088 | tf_op jit(solution)/shard_map/keys_out/ppermute | solution.py:377
  34.8 0.0 collective-permute-done.1.refs_4_
  34.8 0.0 collective-permute-done.2.refs_6_
  34.8 9.0 %all-to-all-done.1.kv_ref = bf16[16,2,2,16,128]{4,3,2,1,0:T(8,128)(2,1)S(1)} async-done(((bf16[16,2,2,16,128]{4,3,2,1,0:T(8,128)(2,1)}), bf16[16,2,2,16,128]{4,3,2,1,0:T(8,128)(2,1)S(1)}, u32[]{:S(2)}, u32[]{:S(2)}) %all-to-all-start.1) | async-done | bytes 262176 | tf_op jit(solution)/shard_map/keys_out/all_to_all | solution.py:381
  43.8 0.0 copy-done.6
  43.8 0.0 copy-done.7
  43.8 0.0 copy-done.8
  43.8 0.0 copy-done.9
  43.8 0.0 copy-done.10
  43.8 0.0 copy-done.11
  43.9 0.0 copy-start.2
  43.9 0.0 copy-start.3
  43.9 0.0 copy-start.1
  43.9 4.3 %attend.1 = (bf16[256,1024]{1,0:T(8,128)(2,1)}, bf16[256,128]{1,0:T(8,128)(2,1)}, bf16[256,128]{1,0:T(8,128)(2,1)}, bf16[16,2,2,16,128]{4,3,2,1,0:T(8,128)(2,1)S(1)}) custom-call(s32[1,32]{1,0:T(1,128)S(1)} %bitcast.16, s32[1,64]{1,0:T(1,128)S(1)} %bitcast.12, s32[1,16]{1,0:T(1,128)S(1)} %bitcast.17, bf16[16,2,2,16,128]{4,3,2,1,0:T(8,128)(2,1)S(1)} %all-to-all-done.1.kv_ref, ...), custom_call_target="tpu_custom_call" | custom-call | flops 1006632960 | bytes 3145728 | tf_op jit(solution)/shard_map/attention/attend/pallas_call | solution.py:269
  48.2 0.0 copy-start
  48.2 16.1 %all_to_all.20.got_ref = bf16[16,2,2,16,128]{4,3,2,1,0:T(8,128)(2,1)S(1)} all-to-all(bf16[16,2,2,16,128]{4,3,2,1,0:T(8,128)(2,1)S(1)} %get-tuple-element.26), channel_id=1, replica_groups=mesh['x_hi'=2,'z'=8,'core'=2,'x_lo'=2,'y'=4] {'x_hi','z'}, dimensions={0} | all-to-all | bytes 524288 | tf_op jit(solution)/shard_map/grads_back/all_to_all | solution.py:381
  64.3 0.3 collect.1
  64.6 0.0 collective-permute-done.3.refs_5_
  64.7 0.1 collective-permute-start.4
  64.8 1.2 %collective-permute-done.4.other_ref = bf16[16,16,128]{2,1,0:T(8,128)(2,1)S(1)} collective-permute-done((bf16[16,16,128]{2,1,0:T(8,128)(2,1)S(1)}, bf16[16,16,128]{2,1,0:T(8,128)(2,1)S(1)}, u32[]{:S(2)}, u32[]{:S(2)}) %collective-permute-start.4) | collective-permute-done | bytes 65568 | tf_op jit(solution)/shard_map/grads_back/ppermute | solution.py:385
  66.0 0.0 copy-done.2
  66.0 0.0 copy-done.3
  66.0 0.2 unkey.1.refs_0_
  66.3 3.1 %collective-permute-start.7 = (bf16[128,256]{1,0:T(8,128)(2,1)S(1)}, bf16[128,256]{1,0:T(8,128)(2,1)S(1)}, u32[]{:S(2)}, u32[]{:S(2)}) collective-permute-start(bf16[128,256]{1,0:T(8,128)(2,1)S(1)} %unkey.1.refs_0_), channel_id=1, source_target_pairs={{0,2},{1,3},{2,0},{3,1},{4,6},{5,7},{6,4},{7,5},{8,10},{9,11},{10,... | collective-permute-start | bytes 196616 | tf_op jit(solution)/shard_map/grads_back/ppermute | solution.py:377
  69.4 1.1 %collective-permute-start.6 = (bf16[128,256]{1,0:T(8,128)(2,1)S(1)}, bf16[128,256]{1,0:T(8,128)(2,1)S(1)}, u32[]{:S(2)}, u32[]{:S(2)}) collective-permute-start(bf16[128,256]{1,0:T(8,128)(2,1)S(1)} %unkey.1.refs_0_), channel_id=1, source_target_pairs={{0,3},{1,2},{2,1},{3,0},{4,7},{5,6},{6,5},{7,4},{8,11},{9,10},{10,... | collective-permute-start | bytes 196616 | tf_op jit(solution)/shard_map/grads_back/ppermute | solution.py:377
  70.5 0.0 collective-permute-start.5
  70.5 1.7 %collective-permute-done.7.refs_3_ = bf16[128,256]{1,0:T(8,128)(2,1)S(1)} collective-permute-done((bf16[128,256]{1,0:T(8,128)(2,1)S(1)}, bf16[128,256]{1,0:T(8,128)(2,1)S(1)}, u32[]{:S(2)}, u32[]{:S(2)}) %collective-permute-start.7) | collective-permute-done | bytes 65568 | tf_op jit(solution)/shard_map/grads_back/ppermute | solution.py:377
  72.1 2.8 %collective-permute-done.6.refs_2_ = bf16[128,256]{1,0:T(8,128)(2,1)S(1)} collective-permute-done((bf16[128,256]{1,0:T(8,128)(2,1)S(1)}, bf16[128,256]{1,0:T(8,128)(2,1)S(1)}, u32[]{:S(2)}, u32[]{:S(2)}) %collective-permute-start.6) | collective-permute-done | bytes 65568 | tf_op jit(solution)/shard_map/grads_back/ppermute | solution.py:377
  74.9 0.0 collective-permute-done.5.refs_1_
  74.9 0.0 copy-done.1
  74.9 0.0 copy-done
  74.9 0.9 input_grad.1
  75.8 17.2 %all_to_all.21 = bf16[32,8,640]{2,1,0:T(8,128)(2,1)S(1)} all-to-all(bf16[32,8,640]{2,1,0:T(8,128)(2,1)S(1)} %bitcast.8), channel_id=1, replica_groups=mesh['x_hi'=2,'z'=8,'core'=2,'x_lo'=2,'y'=4] {'x_lo','x_hi','z'}, dimensions={0} | all-to-all | bytes 655360 | tf_op jit(solution)/shard_map/input_grad/all_to_all | solution.py:413
  93.0 0.7 reduce
Async XLA Ops:
  0.6 26.1 %copy-start.4 = (s32[64]{0:T(128)S(1)}, s32[64]{0:T(128)}, u32[]{:S(2)}) copy-start(s32[64]{0:T(128)} %param.22) | copy-start | bytes 772
  0.6 26.1 %copy-start.5 = (s32[16]{0:T(128)S(1)}, s32[16]{0:T(128)}, u32[]{:S(2)}) copy-start(s32[16]{0:T(128)} %param.23) | copy-start | bytes 196
  4.5 39.3 %copy-start.6 = (bf16[256,1024]{1,0:T(8,128)(2,1)S(1)}, bf16[256,1024]{1,0:T(8,128)(2,1)}, u32[]{:S(2)}) copy-start(bf16[256,1024]{1,0:T(8,128)(2,1)} %q_ref.1) | copy-start | bytes 1572868
  4.5 39.3 %copy-start.7 = (bf16[256,1024]{1,0:T(8,128)(2,1)S(1)}, bf16[256,1024]{1,0:T(8,128)(2,1)}, u32[]{:S(2)}) copy-start(bf16[256,1024]{1,0:T(8,128)(2,1)} %g_ref.1) | copy-start | bytes 1572868
  4.5 39.3 %copy-start.8 = (bf16[256,128]{1,0:T(8,128)(2,1)S(1)}, bf16[256,128]{1,0:T(8,128)(2,1)}, u32[]{:S(2)}) copy-start(bf16[256,128]{1,0:T(8,128)(2,1)} %rk_ref.1) | copy-start | bytes 196612
  4.5 39.3 %copy-start.9 = (bf16[256,128]{1,0:T(8,128)(2,1)S(1)}, bf16[256,128]{1,0:T(8,128)(2,1)}, u32[]{:S(2)}) copy-start(bf16[256,128]{1,0:T(8,128)(2,1)} %rv_ref.1) | copy-start | bytes 196612
  4.5 39.3 %copy-start.10 = (s32[32]{0:T(128)S(1)}, s32[32]{0:T(128)}, u32[]{:S(2)}) copy-start(s32[32]{0:T(128)} %param.21) | copy-start | bytes 388
  4.6 39.3 %copy-start.11 = (s32[16]{0:T(128)S(1)}, s32[16]{0:T(128)}, u32[]{:S(2)}) copy-start(s32[16]{0:T(128)} %param.24) | copy-start | bytes 196
  4.6 20.8 %all-to-all-start = ((bf16[16,32,128]{2,1,0:T(8,128)(2,1)}), bf16[16,32,128]{2,1,0:T(8,128)(2,1)S(1)}, u32[]{:S(2)}, u32[]{:S(2)}) async-start(bf16[16,32,128]{2,1,0:T(8,128)(2,1)} %get-tuple-element.19), calls=%async_computation | async-start | bytes 262144 | tf_op jit(solution)/shard_map/keys_out/all_to_all | solution.py:381
  15.8 19.0 %collective-permute-start.1 = (bf16[2,2,640,128]{3,2,1,0:T(8,128)(2,1)}, bf16[2,2,640,128]{3,2,1,0:T(8,128)(2,1)S(1)}, u32[]{:S(2)}, u32[]{:S(2)}) collective-permute-start(bf16[2,2,640,128]{3,2,1,0:T(8,128)(2,1)} %get-tuple-element.20), channel_id=1, source_target_pairs={{0,1},{1,0},{2,3},{3,2},{4,5},{5,4},{6,7},{7,6},{8,9},{9,8},{10,11... | collective-permute-start | bytes 1966088 | tf_op jit(solution)/shard_map/keys_out/ppermute | solution.py:377
  17.3 17.5 %collective-permute-start.2 = (bf16[2,2,640,128]{3,2,1,0:T(8,128)(2,1)}, bf16[2,2,640,128]{3,2,1,0:T(8,128)(2,1)S(1)}, u32[]{:S(2)}, u32[]{:S(2)}) collective-permute-start(bf16[2,2,640,128]{3,2,1,0:T(8,128)(2,1)} %get-tuple-element.21), channel_id=1, source_target_pairs={{0,3},{1,2},{2,1},{3,0},{4,7},{5,6},{6,5},{7,4},{8,11},{9,10},{10,... | collective-permute-start | bytes 1966088 | tf_op jit(solution)/shard_map/keys_out/ppermute | solution.py:377
  25.4 1.3 %collective-permute-start = (bf16[16,32,128]{2,1,0:T(8,128)(2,1)S(1)}, bf16[16,32,128]{2,1,0:T(8,128)(2,1)S(1)}, u32[]{:S(2)}, u32[]{:S(2)}) collective-permute-start(bf16[16,32,128]{2,1,0:T(8,128)(2,1)S(1)} %all-to-all-done.mine_ref.units_ref), channel_id=1, source_target_pairs={{0,8},{8,0},{1,9},{9,1},{2,10},{10,2},{3,11},{11,3},{4,12},{12,4},... | collective-permute-start | bytes 393224 | tf_op jit(solution)/shard_map/keys_out/ppermute | solution.py:385
  27.7 16.1 %all-to-all-start.1 = ((bf16[16,2,2,16,128]{4,3,2,1,0:T(8,128)(2,1)}), bf16[16,2,2,16,128]{4,3,2,1,0:T(8,128)(2,1)S(1)}, u32[]{:S(2)}, u32[]{:S(2)}) async-start(bf16[16,2,2,16,128]{4,3,2,1,0:T(8,128)(2,1)} %select.1), calls=%async_computation.1 | async-start | bytes 524288 | tf_op jit(solution)/shard_map/keys_out/all_to_all | solution.py:381
  31.6 33.1 %collective-permute-start.3 = (bf16[2,2,640,128]{3,2,1,0:T(8,128)(2,1)}, bf16[2,2,640,128]{3,2,1,0:T(8,128)(2,1)S(1)}, u32[]{:S(2)}, u32[]{:S(2)}) collective-permute-start(bf16[2,2,640,128]{3,2,1,0:T(8,128)(2,1)} %get-tuple-element.29), channel_id=1, source_target_pairs={{0,2},{1,3},{2,0},{3,1},{4,6},{5,7},{6,4},{7,5},{8,10},{9,11},{10,... | collective-permute-start | bytes 1966088 | tf_op jit(solution)/shard_map/keys_out/ppermute | solution.py:377
  43.9 22.2 %copy-start.2 = (f32[2,128,128]{2,1,0:T(8,128)S(1)}, f32[2,128,128]{2,1,0:T(8,128)}, u32[]{:S(2)}) copy-start(f32[2,128,128]{2,1,0:T(8,128)} %constant.4.clone.table_ref) | copy-start | bytes 393220
  43.9 22.1 %copy-start.3 = (f32[128]{0:T(128)S(1)}, f32[128]{0:T(128)}, u32[]{:S(2)}) copy-start(f32[128]{0:T(128)} %param.16) | copy-start | bytes 1540
  43.9 31.0 %copy-start.1 = (bf16[5120,128]{1,0:T(8,128)(2,1)S(1)}, bf16[5120,128]{1,0:T(8,128)(2,1)}, u32[]{:S(2)}) copy-start(bf16[5120,128]{1,0:T(8,128)(2,1)} %wv_ref.3) | copy-start | bytes 3932164
  48.2 26.7 %copy-start = (bf16[5120,128]{1,0:T(8,128)(2,1)S(1)}, bf16[5120,128]{1,0:T(8,128)(2,1)}, u32[]{:S(2)}) copy-start(bf16[5120,128]{1,0:T(8,128)(2,1)} %wk_ref.3) | copy-start | bytes 3932164
  64.7 1.3 %collective-permute-start.4 = (bf16[16,16,128]{2,1,0:T(8,128)(2,1)S(1)}, bf16[16,16,128]{2,1,0:T(8,128)(2,1)S(1)}, u32[]{:S(2)}, u32[]{:S(2)}) collective-permute-start(bf16[16,16,128]{2,1,0:T(8,128)(2,1)S(1)} %get-tuple-element.30), channel_id=1, source_target_pairs={{0,8},{8,0},{1,9},{9,1},{2,10},{10,2},{3,11},{11,3},{4,12},{12,4},... | collective-permute-start | bytes 196616 | tf_op jit(solution)/shard_map/grads_back/ppermute | solution.py:385
  66.3 5.9 %collective-permute-start.7 = (bf16[128,256]{1,0:T(8,128)(2,1)S(1)}, bf16[128,256]{1,0:T(8,128)(2,1)S(1)}, u32[]{:S(2)}, u32[]{:S(2)}) collective-permute-start(bf16[128,256]{1,0:T(8,128)(2,1)S(1)} %unkey.1.refs_0_), channel_id=1, source_target_pairs={{0,2},{1,3},{2,0},{3,1},{4,6},{5,7},{6,4},{7,5},{8,10},{9,11},{10,... | collective-permute-start | bytes 196616 | tf_op jit(solution)/shard_map/grads_back/ppermute | solution.py:377
  69.4 5.5 %collective-permute-start.6 = (bf16[128,256]{1,0:T(8,128)(2,1)S(1)}, bf16[128,256]{1,0:T(8,128)(2,1)S(1)}, u32[]{:S(2)}, u32[]{:S(2)}) collective-permute-start(bf16[128,256]{1,0:T(8,128)(2,1)S(1)} %unkey.1.refs_0_), channel_id=1, source_target_pairs={{0,3},{1,2},{2,1},{3,0},{4,7},{5,6},{6,5},{7,4},{8,11},{9,10},{10,... | collective-permute-start | bytes 196616 | tf_op jit(solution)/shard_map/grads_back/ppermute | solution.py:377
  70.5 4.4 %collective-permute-start.5 = (bf16[128,256]{1,0:T(8,128)(2,1)S(1)}, bf16[128,256]{1,0:T(8,128)(2,1)S(1)}, u32[]{:S(2)}, u32[]{:S(2)}) collective-permute-start(bf16[128,256]{1,0:T(8,128)(2,1)S(1)} %unkey.1.refs_0_), channel_id=1, source_target_pairs={{0,1},{1,0},{2,3},{3,2},{4,5},{5,4},{6,7},{7,6},{8,9},{9,8},{10,11... | collective-permute-start | bytes 196616 | tf_op jit(solution)/shard_map/grads_back/ppermute | solution.py:377

commit v4 on v3

--- a/solution.py
+++ b/solution.py
@@ -233,9 +233,10 @@
     drk_ref[...] = dk[PLEN:].astype(bf16)
     drv_ref[...] = dv[PLEN:].astype(bf16)
     keys_t = keys.T
-    for h in range(GROUPS):
-        cols = slice(h * HEAD, (h + 1) * HEAD)
-        dq_ref[:, cols] = kept((dot_nn(keys_t, ds_s[:, cols]) * SCALE).T).astype(bf16)
+    for h in range(0, GROUPS, PAIRS):
+        d_q = kept(dot_nn(keys_t, ds_s[:, h * HEAD:(h + PAIRS) * HEAD]) * SCALE)
+        for i in range(PAIRS):
+            dq_ref[:, (h + i) * HEAD:(h + i + 1) * HEAD] = d_q[:, i * HEAD:(i + 1) * HEAD].T.astype(bf16)
 
 
 def entry(ref, index):

time: 94.1 us -> 93.8 us (level)
  no operation moved by 1% of the time
where the time goes in v4:
time: 93.8 us; the launch traced here: 93.4 us
  blocking collectives  33.3 us (36%)
  starting transfers between devices  26.3 us (28%)
  waiting for transfers between devices  21.9 us (23%)
  Pallas kernels  10.3 us (11%)
    all_to_all x1, blocking collectives, on_device(): shares = lax.all_to_all(shares, ('x_lo',) + SPREAD, 0, 0, tiled=True)  17.2 us
    all_to_all x1, blocking collectives, spread(): return lax.all_to_all(x, SPREAD, 0, 0, tiled=True)  16.1 us
    all_to_all x2, starting transfers between devices, spread(): return lax.all_to_all(x, SPREAD, 0, 0, tiled=True)  15.1 us
    all_to_all x2, waiting for transfers between devices, spread(): return lax.all_to_all(x, SPREAD, 0, 0, tiled=True)  14.9 us
    ppermute x6, starting transfers between devices, swap_y(): return lax.ppermute(x, 'y', [(i, i ^ k) for i in range(Y)])  11.2 us
    ppermute x6, waiting for transfers between devices, swap_y(): return lax.ppermute(x, 'y', [(i, i ^ k) for i in range(Y)])  4.44 us
    pallas_call x1, Pallas kernels, attend(): pl.pallas_call(attend_kernel, in_specs=[vmem] * 8, out_specs=[vmem] * 4,...  4.02 us
    pallas_call x1, Pallas kernels, project(): pl.pallas_call(project_kernel, in_specs=[hbm] * 5, out_specs=[vmem] + [an...  3.84 us
  transfers between devices with their start and end apart: 10, of which 6 were waited for; matrix products, arithmetic and copies ran while one was open for 0% of the time, Pallas kernels for 6%

profile of v4, /device:TPU:32, one launch (start us, length us, event | category | flops | bytes accessed | tf_op | source)
XLA Modules:
  0.0 93.4 jit_solution(10396099660496632912)
XLA Ops:
  0.6 0.0 copy-start.4
  0.6 0.0 copy-start.5
  0.7 3.8 %project.1 = (bf16[16,32,128]{2,1,0:T(8,128)(2,1)}, bf16[2,2,640,128]{3,2,1,0:T(8,128)(2,1)}, bf16[2,2,640,128]{3,2,1,0:T(8,128)(2,1)}, bf16[2,2,640,128]{3,2,1,0:T(8,128)(2,1)}) custom-call(bf16[128,5120]{1,0:T(8,128)(2,1)} %x_ref.1, bf16[5120,128]{1,0:T(8,128)(2,1)} %wk_ref.3, bf16[5120,128]{1,0:T(8,128)(2,1)} %wv_ref.3, f32[1,128]{1,0:T(1,128)} %bitcast.9, ...), custom_call_target="tpu_custom_call" | custom-call | flops 335544320 | bytes 4194304 | tf_op jit(solution)/shard_map/keys_out/project/pallas_call | solution.py:135
  4.5 0.0 copy-start.6
  4.5 0.0 copy-start.7
  4.5 0.0 copy-start.8
  4.5 0.0 copy-start.9
  4.5 0.0 copy-start.10
  4.6 0.0 copy-start.11
  4.6 11.2 %all-to-all-start = ((bf16[16,32,128]{2,1,0:T(8,128)(2,1)}), bf16[16,32,128]{2,1,0:T(8,128)(2,1)S(1)}, u32[]{:S(2)}, u32[]{:S(2)}) async-start(bf16[16,32,128]{2,1,0:T(8,128)(2,1)} %get-tuple-element.19), calls=%async_computation | async-start | bytes 262144 | tf_op jit(solution)/shard_map/keys_out/all_to_all | solution.py:382
  15.8 1.6 %collective-permute-start.1 = (bf16[2,2,640,128]{3,2,1,0:T(8,128)(2,1)}, bf16[2,2,640,128]{3,2,1,0:T(8,128)(2,1)S(1)}, u32[]{:S(2)}, u32[]{:S(2)}) collective-permute-start(bf16[2,2,640,128]{3,2,1,0:T(8,128)(2,1)} %get-tuple-element.20), channel_id=1, source_target_pairs={{0,1},{1,0},{2,3},{3,2},{4,5},{5,4},{6,7},{7,6},{8,9},{9,8},{10,11... | collective-permute-start | bytes 1966088 | tf_op jit(solution)/shard_map/keys_out/ppermute | solution.py:378
  17.3 2.2 %collective-permute-start.2 = (bf16[2,2,640,128]{3,2,1,0:T(8,128)(2,1)}, bf16[2,2,640,128]{3,2,1,0:T(8,128)(2,1)S(1)}, u32[]{:S(2)}, u32[]{:S(2)}) collective-permute-start(bf16[2,2,640,128]{3,2,1,0:T(8,128)(2,1)} %get-tuple-element.21), channel_id=1, source_target_pairs={{0,3},{1,2},{2,1},{3,0},{4,7},{5,6},{6,5},{7,4},{8,11},{9,10},{10,... | collective-permute-start | bytes 1966088 | tf_op jit(solution)/shard_map/keys_out/ppermute | solution.py:378
  19.5 5.8 %all-to-all-done.mine_ref.units_ref = bf16[16,32,128]{2,1,0:T(8,128)(2,1)S(1)} async-done(((bf16[16,32,128]{2,1,0:T(8,128)(2,1)}), bf16[16,32,128]{2,1,0:T(8,128)(2,1)S(1)}, u32[]{:S(2)}, u32[]{:S(2)}) %all-to-all-start) | async-done | bytes 131104 | tf_op jit(solution)/shard_map/keys_out/all_to_all | solution.py:382
  25.4 0.0 collective-permute-start
  25.4 1.3 %collective-permute-done.other_ref = bf16[16,32,128]{2,1,0:T(8,128)(2,1)S(1)} collective-permute-done((bf16[16,32,128]{2,1,0:T(8,128)(2,1)S(1)}, bf16[16,32,128]{2,1,0:T(8,128)(2,1)S(1)}, u32[]{:S(2)}, u32[]{:S(2)}) %collective-permute-start) | collective-permute-done | bytes 131104 | tf_op jit(solution)/shard_map/keys_out/ppermute | solution.py:386
  26.7 0.0 copy-done.4
  26.7 0.0 copy-done.5
  26.7 1.0 %select.1 = bf16[16,2,2,16,128]{4,3,2,1,0:T(8,128)(2,1)} custom-call(s32[1,64]{1,0:T(1,128)S(1)} %bitcast.11, s32[1,16]{1,0:T(1,128)S(1)} %bitcast.14, bf16[16,32,128]{2,1,0:T(8,128)(2,1)S(1)} %all-to-all-done.mine_ref.units_ref, bf16[16,32,128]{2,1,0:T(8,128)(2,1)S(1)} %collective-permute-done.other_ref), custom_call_target="tpu_custom_call" | custom-call | tf_op jit(solution)/shard_map/keys_out/select/pallas_call | solution.py:185
  27.7 3.9 %all-to-all-start.1 = ((bf16[16,2,2,16,128]{4,3,2,1,0:T(8,128)(2,1)}), bf16[16,2,2,16,128]{4,3,2,1,0:T(8,128)(2,1)S(1)}, u32[]{:S(2)}, u32[]{:S(2)}) async-start(bf16[16,2,2,16,128]{4,3,2,1,0:T(8,128)(2,1)} %select.1), calls=%async_computation.1 | async-start | bytes 524288 | tf_op jit(solution)/shard_map/keys_out/all_to_all | solution.py:382
  31.6 3.2 %collective-permute-start.3 = (bf16[2,2,640,128]{3,2,1,0:T(8,128)(2,1)}, bf16[2,2,640,128]{3,2,1,0:T(8,128)(2,1)S(1)}, u32[]{:S(2)}, u32[]{:S(2)}) collective-permute-start(bf16[2,2,640,128]{3,2,1,0:T(8,128)(2,1)} %get-tuple-element.29), channel_id=1, source_target_pairs={{0,2},{1,3},{2,0},{3,1},{4,6},{5,7},{6,4},{7,5},{8,10},{9,11},{10,... | collective-permute-start | bytes 1966088 | tf_op jit(solution)/shard_map/keys_out/ppermute | solution.py:378
  34.8 0.0 collective-permute-done.1.refs_4_
  34.8 0.0 collective-permute-done.2.refs_6_
  34.8 9.0 %all-to-all-done.1.kv_ref = bf16[16,2,2,16,128]{4,3,2,1,0:T(8,128)(2,1)S(1)} async-done(((bf16[16,2,2,16,128]{4,3,2,1,0:T(8,128)(2,1)}), bf16[16,2,2,16,128]{4,3,2,1,0:T(8,128)(2,1)S(1)}, u32[]{:S(2)}, u32[]{:S(2)}) %all-to-all-start.1) | async-done | bytes 262176 | tf_op jit(solution)/shard_map/keys_out/all_to_all | solution.py:382
  43.8 0.0 copy-done.6
  43.8 0.0 copy-done.7
  43.8 0.0 copy-done.8
  43.8 0.0 copy-done.9
  43.8 0.0 copy-done.10
  43.8 0.0 copy-done.11
  43.9 0.0 copy-start.2
  43.9 0.0 copy-start.3
  43.9 0.0 copy-start.1
  43.9 4.0 %attend.1 = (bf16[256,1024]{1,0:T(8,128)(2,1)}, bf16[256,128]{1,0:T(8,128)(2,1)}, bf16[256,128]{1,0:T(8,128)(2,1)}, bf16[16,2,2,16,128]{4,3,2,1,0:T(8,128)(2,1)S(1)}) custom-call(s32[1,32]{1,0:T(1,128)S(1)} %bitcast.16, s32[1,64]{1,0:T(1,128)S(1)} %bitcast.12, s32[1,16]{1,0:T(1,128)S(1)} %bitcast.17, bf16[16,2,2,16,128]{4,3,2,1,0:T(8,128)(2,1)S(1)} %all-to-all-done.1.kv_ref, ...), custom_call_target="tpu_custom_call" | custom-call | flops 1006632960 | bytes 3145728 | tf_op jit(solution)/shard_map/attention/attend/pallas_call | solution.py:270
  47.9 0.0 copy-start
  47.9 16.1 %all_to_all.20.got_ref = bf16[16,2,2,16,128]{4,3,2,1,0:T(8,128)(2,1)S(1)} all-to-all(bf16[16,2,2,16,128]{4,3,2,1,0:T(8,128)(2,1)S(1)} %get-tuple-element.26), channel_id=1, replica_groups=mesh['x_hi'=2,'z'=8,'core'=2,'x_lo'=2,'y'=4] {'x_hi','z'}, dimensions={0} | all-to-all | bytes 524288 | tf_op jit(solution)/shard_map/grads_back/all_to_all | solution.py:382
  64.0 0.3 collect.1
  64.4 0.0 collective-permute-done.3.refs_5_
  64.4 0.1 collective-permute-start.4
  64.5 1.2 %collective-permute-done.4.other_ref = bf16[16,16,128]{2,1,0:T(8,128)(2,1)S(1)} collective-permute-done((bf16[16,16,128]{2,1,0:T(8,128)(2,1)S(1)}, bf16[16,16,128]{2,1,0:T(8,128)(2,1)S(1)}, u32[]{:S(2)}, u32[]{:S(2)}) %collective-permute-start.4) | collective-permute-done | bytes 65568 | tf_op jit(solution)/shard_map/grads_back/ppermute | solution.py:386
  65.7 0.0 copy-done.2
  65.7 0.0 copy-done.3
  65.7 0.2 unkey.1.refs_0_
  66.0 3.1 %collective-permute-start.7 = (bf16[128,256]{1,0:T(8,128)(2,1)S(1)}, bf16[128,256]{1,0:T(8,128)(2,1)S(1)}, u32[]{:S(2)}, u32[]{:S(2)}) collective-permute-start(bf16[128,256]{1,0:T(8,128)(2,1)S(1)} %unkey.1.refs_0_), channel_id=1, source_target_pairs={{0,2},{1,3},{2,0},{3,1},{4,6},{5,7},{6,4},{7,5},{8,10},{9,11},{10,... | collective-permute-start | bytes 196616 | tf_op jit(solution)/shard_map/grads_back/ppermute | solution.py:378
  69.1 1.0 %collective-permute-start.6 = (bf16[128,256]{1,0:T(8,128)(2,1)S(1)}, bf16[128,256]{1,0:T(8,128)(2,1)S(1)}, u32[]{:S(2)}, u32[]{:S(2)}) collective-permute-start(bf16[128,256]{1,0:T(8,128)(2,1)S(1)} %unkey.1.refs_0_), channel_id=1, source_target_pairs={{0,3},{1,2},{2,1},{3,0},{4,7},{5,6},{6,5},{7,4},{8,11},{9,10},{10,... | collective-permute-start | bytes 196616 | tf_op jit(solution)/shard_map/grads_back/ppermute | solution.py:378
  70.2 0.0 collective-permute-start.5
  70.2 1.7 %collective-permute-done.7.refs_3_ = bf16[128,256]{1,0:T(8,128)(2,1)S(1)} collective-permute-done((bf16[128,256]{1,0:T(8,128)(2,1)S(1)}, bf16[128,256]{1,0:T(8,128)(2,1)S(1)}, u32[]{:S(2)}, u32[]{:S(2)}) %collective-permute-start.7) | collective-permute-done | bytes 65568 | tf_op jit(solution)/shard_map/grads_back/ppermute | solution.py:378
  71.8 2.8 %collective-permute-done.6.refs_2_ = bf16[128,256]{1,0:T(8,128)(2,1)S(1)} collective-permute-done((bf16[128,256]{1,0:T(8,128)(2,1)S(1)}, bf16[128,256]{1,0:T(8,128)(2,1)S(1)}, u32[]{:S(2)}, u32[]{:S(2)}) %collective-permute-start.6) | collective-permute-done | bytes 65568 | tf_op jit(solution)/shard_map/grads_back/ppermute | solution.py:378
  74.6 0.0 collective-permute-done.5.refs_1_
  74.6 0.0 copy-done.1
  74.6 0.0 copy-done
  74.6 0.9 input_grad.1
  75.5 17.2 %all_to_all.21 = bf16[32,8,640]{2,1,0:T(8,128)(2,1)S(1)} all-to-all(bf16[32,8,640]{2,1,0:T(8,128)(2,1)S(1)} %bitcast.8), channel_id=1, replica_groups=mesh['x_hi'=2,'z'=8,'core'=2,'x_lo'=2,'y'=4] {'x_lo','x_hi','z'}, dimensions={0} | all-to-all | bytes 655360 | tf_op jit(solution)/shard_map/input_grad/all_to_all | solution.py:414
  92.7 0.7 reduce
Async XLA Ops:
  0.6 26.1 %copy-start.4 = (s32[64]{0:T(128)S(1)}, s32[64]{0:T(128)}, u32[]{:S(2)}) copy-start(s32[64]{0:T(128)} %param.22) | copy-start | bytes 772
  0.6 26.1 %copy-start.5 = (s32[16]{0:T(128)S(1)}, s32[16]{0:T(128)}, u32[]{:S(2)}) copy-start(s32[16]{0:T(128)} %param.23) | copy-start | bytes 196
  4.5 39.3 %copy-start.6 = (bf16[256,1024]{1,0:T(8,128)(2,1)S(1)}, bf16[256,1024]{1,0:T(8,128)(2,1)}, u32[]{:S(2)}) copy-start(bf16[256,1024]{1,0:T(8,128)(2,1)} %q_ref.1) | copy-start | bytes 1572868
  4.5 39.3 %copy-start.7 = (bf16[256,1024]{1,0:T(8,128)(2,1)S(1)}, bf16[256,1024]{1,0:T(8,128)(2,1)}, u32[]{:S(2)}) copy-start(bf16[256,1024]{1,0:T(8,128)(2,1)} %g_ref.1) | copy-start | bytes 1572868
  4.5 39.3 %copy-start.8 = (bf16[256,128]{1,0:T(8,128)(2,1)S(1)}, bf16[256,128]{1,0:T(8,128)(2,1)}, u32[]{:S(2)}) copy-start(bf16[256,128]{1,0:T(8,128)(2,1)} %rk_ref.1) | copy-start | bytes 196612
  4.5 39.3 %copy-start.9 = (bf16[256,128]{1,0:T(8,128)(2,1)S(1)}, bf16[256,128]{1,0:T(8,128)(2,1)}, u32[]{:S(2)}) copy-start(bf16[256,128]{1,0:T(8,128)(2,1)} %rv_ref.1) | copy-start | bytes 196612
  4.5 39.3 %copy-start.10 = (s32[32]{0:T(128)S(1)}, s32[32]{0:T(128)}, u32[]{:S(2)}) copy-start(s32[32]{0:T(128)} %param.21) | copy-start | bytes 388
  4.6 39.3 %copy-start.11 = (s32[16]{0:T(128)S(1)}, s32[16]{0:T(128)}, u32[]{:S(2)}) copy-start(s32[16]{0:T(128)} %param.24) | copy-start | bytes 196
  4.6 20.8 %all-to-all-start = ((bf16[16,32,128]{2,1,0:T(8,128)(2,1)}), bf16[16,32,128]{2,1,0:T(8,128)(2,1)S(1)}, u32[]{:S(2)}, u32[]{:S(2)}) async-start(bf16[16,32,128]{2,1,0:T(8,128)(2,1)} %get-tuple-element.19), calls=%async_computation | async-start | bytes 262144 | tf_op jit(solution)/shard_map/keys_out/all_to_all | solution.py:382
  15.8 19.0 %collective-permute-start.1 = (bf16[2,2,640,128]{3,2,1,0:T(8,128)(2,1)}, bf16[2,2,640,128]{3,2,1,0:T(8,128)(2,1)S(1)}, u32[]{:S(2)}, u32[]{:S(2)}) collective-permute-start(bf16[2,2,640,128]{3,2,1,0:T(8,128)(2,1)} %get-tuple-element.20), channel_id=1, source_target_pairs={{0,1},{1,0},{2,3},{3,2},{4,5},{5,4},{6,7},{7,6},{8,9},{9,8},{10,11... | collective-permute-start | bytes 1966088 | tf_op jit(solution)/shard_map/keys_out/ppermute | solution.py:378
  17.3 17.5 %collective-permute-start.2 = (bf16[2,2,640,128]{3,2,1,0:T(8,128)(2,1)}, bf16[2,2,640,128]{3,2,1,0:T(8,128)(2,1)S(1)}, u32[]{:S(2)}, u32[]{:S(2)}) collective-permute-start(bf16[2,2,640,128]{3,2,1,0:T(8,128)(2,1)} %get-tuple-element.21), channel_id=1, source_target_pairs={{0,3},{1,2},{2,1},{3,0},{4,7},{5,6},{6,5},{7,4},{8,11},{9,10},{10,... | collective-permute-start | bytes 1966088 | tf_op jit(solution)/shard_map/keys_out/ppermute | solution.py:378
  25.4 1.3 %collective-permute-start = (bf16[16,32,128]{2,1,0:T(8,128)(2,1)S(1)}, bf16[16,32,128]{2,1,0:T(8,128)(2,1)S(1)}, u32[]{:S(2)}, u32[]{:S(2)}) collective-permute-start(bf16[16,32,128]{2,1,0:T(8,128)(2,1)S(1)} %all-to-all-done.mine_ref.units_ref), channel_id=1, source_target_pairs={{0,8},{8,0},{1,9},{9,1},{2,10},{10,2},{3,11},{11,3},{4,12},{12,4},... | collective-permute-start | bytes 393224 | tf_op jit(solution)/shard_map/keys_out/ppermute | solution.py:386
  27.7 16.1 %all-to-all-start.1 = ((bf16[16,2,2,16,128]{4,3,2,1,0:T(8,128)(2,1)}), bf16[16,2,2,16,128]{4,3,2,1,0:T(8,128)(2,1)S(1)}, u32[]{:S(2)}, u32[]{:S(2)}) async-start(bf16[16,2,2,16,128]{4,3,2,1,0:T(8,128)(2,1)} %select.1), calls=%async_computation.1 | async-start | bytes 524288 | tf_op jit(solution)/shard_map/keys_out/all_to_all | solution.py:382
  31.6 32.8 %collective-permute-start.3 = (bf16[2,2,640,128]{3,2,1,0:T(8,128)(2,1)}, bf16[2,2,640,128]{3,2,1,0:T(8,128)(2,1)S(1)}, u32[]{:S(2)}, u32[]{:S(2)}) collective-permute-start(bf16[2,2,640,128]{3,2,1,0:T(8,128)(2,1)} %get-tuple-element.29), channel_id=1, source_target_pairs={{0,2},{1,3},{2,0},{3,1},{4,6},{5,7},{6,4},{7,5},{8,10},{9,11},{10,... | collective-permute-start | bytes 1966088 | tf_op jit(solution)/shard_map/keys_out/ppermute | solution.py:378
  43.9 21.9 %copy-start.2 = (f32[2,128,128]{2,1,0:T(8,128)S(1)}, f32[2,128,128]{2,1,0:T(8,128)}, u32[]{:S(2)}) copy-start(f32[2,128,128]{2,1,0:T(8,128)} %constant.4.clone.table_ref) | copy-start | bytes 393220
  43.9 21.9 %copy-start.3 = (f32[128]{0:T(128)S(1)}, f32[128]{0:T(128)}, u32[]{:S(2)}) copy-start(f32[128]{0:T(128)} %param.16) | copy-start | bytes 1540
  43.9 30.7 %copy-start.1 = (bf16[5120,128]{1,0:T(8,128)(2,1)S(1)}, bf16[5120,128]{1,0:T(8,128)(2,1)}, u32[]{:S(2)}) copy-start(bf16[5120,128]{1,0:T(8,128)(2,1)} %wv_ref.3) | copy-start | bytes 3932164
  47.9 26.7 %copy-start = (bf16[5120,128]{1,0:T(8,128)(2,1)S(1)}, bf16[5120,128]{1,0:T(8,128)(2,1)}, u32[]{:S(2)}) copy-start(bf16[5120,128]{1,0:T(8,128)(2,1)} %wk_ref.3) | copy-start | bytes 3932164
  64.4 1.3 %collective-permute-start.4 = (bf16[16,16,128]{2,1,0:T(8,128)(2,1)S(1)}, bf16[16,16,128]{2,1,0:T(8,128)(2,1)S(1)}, u32[]{:S(2)}, u32[]{:S(2)}) collective-permute-start(bf16[16,16,128]{2,1,0:T(8,128)(2,1)S(1)} %get-tuple-element.30), channel_id=1, source_target_pairs={{0,8},{8,0},{1,9},{9,1},{2,10},{10,2},{3,11},{11,3},{4,12},{12,4},... | collective-permute-start | bytes 196616 | tf_op jit(solution)/shard_map/grads_back/ppermute | solution.py:386
  66.0 5.9 %collective-permute-start.7 = (bf16[128,256]{1,0:T(8,128)(2,1)S(1)}, bf16[128,256]{1,0:T(8,128)(2,1)S(1)}, u32[]{:S(2)}, u32[]{:S(2)}) collective-permute-start(bf16[128,256]{1,0:T(8,128)(2,1)S(1)} %unkey.1.refs_0_), channel_id=1, source_target_pairs={{0,2},{1,3},{2,0},{3,1},{4,6},{5,7},{6,4},{7,5},{8,10},{9,11},{10,... | collective-permute-start | bytes 196616 | tf_op jit(solution)/shard_map/grads_back/ppermute | solution.py:378
  69.1 5.5 %collective-permute-start.6 = (bf16[128,256]{1,0:T(8,128)(2,1)S(1)}, bf16[128,256]{1,0:T(8,128)(2,1)S(1)}, u32[]{:S(2)}, u32[]{:S(2)}) collective-permute-start(bf16[128,256]{1,0:T(8,128)(2,1)S(1)} %unkey.1.refs_0_), channel_id=1, source_target_pairs={{0,3},{1,2},{2,1},{3,0},{4,7},{5,6},{6,5},{7,4},{8,11},{9,10},{10,... | collective-permute-start | bytes 196616 | tf_op jit(solution)/shard_map/grads_back/ppermute | solution.py:378
  70.2 4.4 %collective-permute-start.5 = (bf16[128,256]{1,0:T(8,128)(2,1)S(1)}, bf16[128,256]{1,0:T(8,128)(2,1)S(1)}, u32[]{:S(2)}, u32[]{:S(2)}) collective-permute-start(bf16[128,256]{1,0:T(8,128)(2,1)S(1)} %unkey.1.refs_0_), channel_id=1, source_target_pairs={{0,1},{1,0},{2,3},{3,2},{4,5},{5,4},{6,7},{7,6},{8,9},{9,8},{10,11... | collective-permute-start | bytes 196616 | tf_op jit(solution)/shard_map/grads_back/ppermute | solution.py:378

commit v5 on v4

--- a/solution.py
+++ b/solution.py
@@ -344,29 +344,47 @@
     )(sums, other, units, gain, table)
 
 
-def input_grad_kernel(wk_ref, wv_ref, *refs):
-    grads, got, out_ref = refs[:Y], refs[Y:2 * Y - 1], refs[-1]
+def own_share_kernel(wk_ref, wv_ref, grads_ref, out_ref):
     y = lax.axis_index("y")
     for half in range(X_LO):
         rows = pl.ds(pl.multiple_of((half * Y + y) * COLS, COLS), COLS)
-        total = dot_nt(grads[0][...], jnp.concatenate([wk_ref[rows], wv_ref[rows]], axis=1))
+        w = jnp.concatenate([wk_ref[rows], wv_ref[rows]], axis=1)
+        out_ref[half] = dot_nt(grads_ref[...], w)
+
+
+def own_share(wk, wv, grads):
+    vmem = pl.BlockSpec(memory_space=pltpu.VMEM)
+    return pl.pallas_call(
+        own_share_kernel,
+        in_specs=[vmem] * 3,
+        out_specs=vmem,
+        out_shape=jax.ShapeDtypeStruct((X_LO, HALF, COLS), f32),
+        compiler_params=pltpu.CompilerParams(vmem_limit_bytes=16 << 20),
+        name="own_share",
+    )(wk, wv, grads)
+
+
+def input_grad_kernel(own_ref, *refs):
+    grads, got, out_ref = refs[:Y - 1], refs[Y - 1:-1], refs[-1]
+    for half in range(X_LO):
+        total = own_ref[half]
         for k in range(1, Y):
             w = jnp.concatenate([got[k - 1][half, 0], got[k - 1][half, 1]], axis=1)
-            total += dot_nt(grads[1 + LAST_FAR.index(k)][...], w)
+            total += dot_nt(grads[LAST_FAR.index(k)][...], w)
         out_ref[half] = total.reshape(CHIPS, PIECE, COLS).astype(bf16)
 
 
-def input_grad(wk, wv, grads, got):
+def input_grad(own, grads, got):
     vmem = pl.BlockSpec(memory_space=pltpu.VMEM)
     return pl.pallas_call(
         input_grad_kernel,
-        in_specs=[vmem] * (2 * Y + 1),
+        in_specs=[vmem] * (2 * Y - 1),
         out_specs=vmem,
         out_shape=jax.ShapeDtypeStruct((X_LO, CHIPS, PIECE, COLS), bf16),
         compiler_params=pltpu.CompilerParams(vmem_limit_bytes=16 << 20),
         cost_estimate=pl.CostEstimate(flops=2 * HALF * WIDTH * 256, bytes_accessed=4 << 20, transcendentals=0),
         name="input_grad",
-    )(wk, wv, *grads, *got)
+    )(own, *grads, *got)
 
 
 def together(first, second):
@@ -407,9 +425,10 @@
         sums, other = collect(slot_prompt, prompt_owner, spread(grads))
         other, got[1] = together(other, got[1])
         both = unkey(sums, swap_cores(other), mine, gain, table)
-        both = [both] + [swap_y(both, k) for k in LAST_FAR]
+        others = [swap_y(both, k) for k in LAST_FAR]
+        own = own_share(key_matrix, value_matrix, both)
     with jax.named_scope("input_grad"):
-        shares = input_grad(key_matrix, value_matrix, both, got)
+        shares = input_grad(own, others, got)
         shares = shares.reshape(X_LO * CHIPS, PIECE, COLS)
         shares = lax.all_to_all(shares, ("x_lo",) + SPREAD, 0, 0, tiled=True)
         shares = shares.reshape(X_LO, CHIPS, PIECE, COLS).astype(f32)

time: 93.8 us -> 93.7 us (level)
  no operation moved by 1% of the time
where the time goes in v5:
time: 93.7 us; the launch traced here: 93.3 us
  blocking collectives  33.3 us (36%)
  starting transfers between devices  26.3 us (28%)
  waiting for transfers between devices  21.5 us (23%)
  Pallas kernels  10.5 us (11%)
    all_to_all x1, blocking collectives, on_device(): shares = lax.all_to_all(shares, ('x_lo',) + SPREAD, 0, 0, tiled=True)  17.2 us
    all_to_all x1, blocking collectives, spread(): return lax.all_to_all(x, SPREAD, 0, 0, tiled=True)  16.1 us
    all_to_all x2, starting transfers between devices, spread(): return lax.all_to_all(x, SPREAD, 0, 0, tiled=True)  15.1 us
    all_to_all x2, waiting for transfers between devices, spread(): return lax.all_to_all(x, SPREAD, 0, 0, tiled=True)  14.9 us
    ppermute x6, starting transfers between devices, swap_y(): return lax.ppermute(x, 'y', [(i, i ^ k) for i in range(Y)])  11.2 us
    ppermute x6, waiting for transfers between devices, swap_y(): return lax.ppermute(x, 'y', [(i, i ^ k) for i in range(Y)])  4.09 us
    pallas_call x1, Pallas kernels, attend(): pl.pallas_call(attend_kernel, in_specs=[vmem] * 8, out_specs=[vmem] * 4,...  4.02 us
    pallas_call x1, Pallas kernels, project(): pl.pallas_call(project_kernel, in_specs=[hbm] * 5, out_specs=[vmem] + [an...  3.84 us
  transfers between devices with their start and end apart: 10, of which 6 were waited for; matrix products, arithmetic and copies ran while one was open for 0% of the time, Pallas kernels for 6%

profile of v5, /device:TPU:32, one launch (start us, length us, event | category | flops | bytes accessed | tf_op | source)
XLA Modules:
  0.0 93.3 jit_solution(9434785737130258363)
XLA Ops:
  0.6 0.0 copy-start.4
  0.6 0.0 copy-start.5
  0.7 3.8 %project.1 = (bf16[16,32,128]{2,1,0:T(8,128)(2,1)}, bf16[2,2,640,128]{3,2,1,0:T(8,128)(2,1)}, bf16[2,2,640,128]{3,2,1,0:T(8,128)(2,1)}, bf16[2,2,640,128]{3,2,1,0:T(8,128)(2,1)}) custom-call(bf16[128,5120]{1,0:T(8,128)(2,1)} %x_ref.1, bf16[5120,128]{1,0:T(8,128)(2,1)} %wk_ref.3, bf16[5120,128]{1,0:T(8,128)(2,1)} %wv_ref.3, f32[1,128]{1,0:T(1,128)} %bitcast.9, ...), custom_call_target="tpu_custom_call" | custom-call | flops 335544320 | bytes 4194304 | tf_op jit(solution)/shard_map/keys_out/project/pallas_call | solution.py:135
  4.5 0.0 copy-start.6
  4.5 0.0 copy-start.7
  4.5 0.0 copy-start.8
  4.5 0.0 copy-start.9
  4.5 0.0 copy-start.10
  4.6 0.0 copy-start.11
  4.6 11.2 %all-to-all-start = ((bf16[16,32,128]{2,1,0:T(8,128)(2,1)}), bf16[16,32,128]{2,1,0:T(8,128)(2,1)S(1)}, u32[]{:S(2)}, u32[]{:S(2)}) async-start(bf16[16,32,128]{2,1,0:T(8,128)(2,1)} %get-tuple-element.19), calls=%async_computation | async-start | bytes 262144 | tf_op jit(solution)/shard_map/keys_out/all_to_all | solution.py:400
  15.8 1.6 %collective-permute-start.1 = (bf16[2,2,640,128]{3,2,1,0:T(8,128)(2,1)}, bf16[2,2,640,128]{3,2,1,0:T(8,128)(2,1)S(1)}, u32[]{:S(2)}, u32[]{:S(2)}) collective-permute-start(bf16[2,2,640,128]{3,2,1,0:T(8,128)(2,1)} %get-tuple-element.20), channel_id=1, source_target_pairs={{0,1},{1,0},{2,3},{3,2},{4,5},{5,4},{6,7},{7,6},{8,9},{9,8},{10,11... | collective-permute-start | bytes 1966088 | tf_op jit(solution)/shard_map/keys_out/ppermute | solution.py:396
  17.3 2.2 %collective-permute-start.2 = (bf16[2,2,640,128]{3,2,1,0:T(8,128)(2,1)}, bf16[2,2,640,128]{3,2,1,0:T(8,128)(2,1)S(1)}, u32[]{:S(2)}, u32[]{:S(2)}) collective-permute-start(bf16[2,2,640,128]{3,2,1,0:T(8,128)(2,1)} %get-tuple-element.21), channel_id=1, source_target_pairs={{0,3},{1,2},{2,1},{3,0},{4,7},{5,6},{6,5},{7,4},{8,11},{9,10},{10,... | collective-permute-start | bytes 1966088 | tf_op jit(solution)/shard_map/keys_out/ppermute | solution.py:396
  19.5 5.8 %all-to-all-done.mine_ref.units_ref = bf16[16,32,128]{2,1,0:T(8,128)(2,1)S(1)} async-done(((bf16[16,32,128]{2,1,0:T(8,128)(2,1)}), bf16[16,32,128]{2,1,0:T(8,128)(2,1)S(1)}, u32[]{:S(2)}, u32[]{:S(2)}) %all-to-all-start) | async-done | bytes 131104 | tf_op jit(solution)/shard_map/keys_out/all_to_all | solution.py:400
  25.4 0.0 collective-permute-start
  25.4 1.3 %collective-permute-done.other_ref = bf16[16,32,128]{2,1,0:T(8,128)(2,1)S(1)} collective-permute-done((bf16[16,32,128]{2,1,0:T(8,128)(2,1)S(1)}, bf16[16,32,128]{2,1,0:T(8,128)(2,1)S(1)}, u32[]{:S(2)}, u32[]{:S(2)}) %collective-permute-start) | collective-permute-done | bytes 131104 | tf_op jit(solution)/shard_map/keys_out/ppermute | solution.py:404
  26.7 0.0 copy-done.4
  26.7 0.0 copy-done.5
  26.7 1.0 %select.1 = bf16[16,2,2,16,128]{4,3,2,1,0:T(8,128)(2,1)} custom-call(s32[1,64]{1,0:T(1,128)S(1)} %bitcast.11, s32[1,16]{1,0:T(1,128)S(1)} %bitcast.14, bf16[16,32,128]{2,1,0:T(8,128)(2,1)S(1)} %all-to-all-done.mine_ref.units_ref, bf16[16,32,128]{2,1,0:T(8,128)(2,1)S(1)} %collective-permute-done.other_ref), custom_call_target="tpu_custom_call" | custom-call | tf_op jit(solution)/shard_map/keys_out/select/pallas_call | solution.py:185
  27.7 3.9 %all-to-all-start.1 = ((bf16[16,2,2,16,128]{4,3,2,1,0:T(8,128)(2,1)}), bf16[16,2,2,16,128]{4,3,2,1,0:T(8,128)(2,1)S(1)}, u32[]{:S(2)}, u32[]{:S(2)}) async-start(bf16[16,2,2,16,128]{4,3,2,1,0:T(8,128)(2,1)} %select.1), calls=%async_computation.1 | async-start | bytes 524288 | tf_op jit(solution)/shard_map/keys_out/all_to_all | solution.py:400
  31.6 3.2 %collective-permute-start.3 = (bf16[2,2,640,128]{3,2,1,0:T(8,128)(2,1)}, bf16[2,2,640,128]{3,2,1,0:T(8,128)(2,1)S(1)}, u32[]{:S(2)}, u32[]{:S(2)}) collective-permute-start(bf16[2,2,640,128]{3,2,1,0:T(8,128)(2,1)} %get-tuple-element.29), channel_id=1, source_target_pairs={{0,2},{1,3},{2,0},{3,1},{4,6},{5,7},{6,4},{7,5},{8,10},{9,11},{10,... | collective-permute-start | bytes 1966088 | tf_op jit(solution)/shard_map/keys_out/ppermute | solution.py:396
  34.8 0.0 collective-permute-done.1.refs_3_
  34.8 0.0 collective-permute-done.2.refs_5_
  34.8 9.0 %all-to-all-done.1.kv_ref = bf16[16,2,2,16,128]{4,3,2,1,0:T(8,128)(2,1)S(1)} async-done(((bf16[16,2,2,16,128]{4,3,2,1,0:T(8,128)(2,1)}), bf16[16,2,2,16,128]{4,3,2,1,0:T(8,128)(2,1)S(1)}, u32[]{:S(2)}, u32[]{:S(2)}) %all-to-all-start.1) | async-done | bytes 262176 | tf_op jit(solution)/shard_map/keys_out/all_to_all | solution.py:400
  43.8 0.0 copy-done.6
  43.8 0.0 copy-done.7
  43.8 0.0 copy-done.8
  43.8 0.0 copy-done.9
  43.8 0.0 copy-done.10
  43.8 0.0 copy-done.11
  43.9 0.0 copy-start.2
  43.9 0.0 copy-start.3
  43.9 0.0 copy-start.1
  43.9 4.0 %attend.1 = (bf16[256,1024]{1,0:T(8,128)(2,1)}, bf16[256,128]{1,0:T(8,128)(2,1)}, bf16[256,128]{1,0:T(8,128)(2,1)}, bf16[16,2,2,16,128]{4,3,2,1,0:T(8,128)(2,1)S(1)}) custom-call(s32[1,32]{1,0:T(1,128)S(1)} %bitcast.16, s32[1,64]{1,0:T(1,128)S(1)} %bitcast.12, s32[1,16]{1,0:T(1,128)S(1)} %bitcast.17, bf16[16,2,2,16,128]{4,3,2,1,0:T(8,128)(2,1)S(1)} %all-to-all-done.1.kv_ref, ...), custom_call_target="tpu_custom_call" | custom-call | flops 1006632960 | bytes 3145728 | tf_op jit(solution)/shard_map/attention/attend/pallas_call | solution.py:270
  47.9 0.0 copy-start
  47.9 16.1 %all_to_all.20.got_ref = bf16[16,2,2,16,128]{4,3,2,1,0:T(8,128)(2,1)S(1)} all-to-all(bf16[16,2,2,16,128]{4,3,2,1,0:T(8,128)(2,1)S(1)} %get-tuple-element.26), channel_id=1, replica_groups=mesh['x_hi'=2,'z'=8,'core'=2,'x_lo'=2,'y'=4] {'x_hi','z'}, dimensions={0} | all-to-all | bytes 524288 | tf_op jit(solution)/shard_map/grads_back/all_to_all | solution.py:400
  64.0 0.3 collect.1
  64.4 0.0 collective-permute-done.3.refs_4_
  64.4 0.1 collective-permute-start.4
  64.5 1.2 %collective-permute-done.4.other_ref = bf16[16,16,128]{2,1,0:T(8,128)(2,1)S(1)} collective-permute-done((bf16[16,16,128]{2,1,0:T(8,128)(2,1)S(1)}, bf16[16,16,128]{2,1,0:T(8,128)(2,1)S(1)}, u32[]{:S(2)}, u32[]{:S(2)}) %collective-permute-start.4) | collective-permute-done | bytes 65568 | tf_op jit(solution)/shard_map/grads_back/ppermute | solution.py:404
  65.7 0.0 copy-done.2
  65.7 0.0 copy-done.3
  65.7 0.2 unkey.1.grads_ref
  66.0 3.1 %collective-permute-start.7 = (bf16[128,256]{1,0:T(8,128)(2,1)S(1)}, bf16[128,256]{1,0:T(8,128)(2,1)S(1)}, u32[]{:S(2)}, u32[]{:S(2)}) collective-permute-start(bf16[128,256]{1,0:T(8,128)(2,1)S(1)} %unkey.1.grads_ref), channel_id=1, source_target_pairs={{0,2},{1,3},{2,0},{3,1},{4,6},{5,7},{6,4},{7,5},{8,10},{9,11},{10,... | collective-permute-start | bytes 196616 | tf_op jit(solution)/shard_map/grads_back/ppermute | solution.py:396
  69.1 1.0 %collective-permute-start.6 = (bf16[128,256]{1,0:T(8,128)(2,1)S(1)}, bf16[128,256]{1,0:T(8,128)(2,1)S(1)}, u32[]{:S(2)}, u32[]{:S(2)}) collective-permute-start(bf16[128,256]{1,0:T(8,128)(2,1)S(1)} %unkey.1.grads_ref), channel_id=1, source_target_pairs={{0,3},{1,2},{2,1},{3,0},{4,7},{5,6},{6,5},{7,4},{8,11},{9,10},{10,... | collective-permute-start | bytes 196616 | tf_op jit(solution)/shard_map/grads_back/ppermute | solution.py:396
  70.2 0.0 collective-permute-start.5
  70.2 0.0 copy-done.1
  70.2 0.0 copy-done
  70.2 0.3 own_share.1.own_ref
  70.5 1.3 %collective-permute-done.7.refs_2_ = bf16[128,256]{1,0:T(8,128)(2,1)S(1)} collective-permute-done((bf16[128,256]{1,0:T(8,128)(2,1)S(1)}, bf16[128,256]{1,0:T(8,128)(2,1)S(1)}, u32[]{:S(2)}, u32[]{:S(2)}) %collective-permute-start.7) | collective-permute-done | bytes 65568 | tf_op jit(solution)/shard_map/grads_back/ppermute | solution.py:396
  71.8 2.8 %collective-permute-done.6.refs_1_ = bf16[128,256]{1,0:T(8,128)(2,1)S(1)} collective-permute-done((bf16[128,256]{1,0:T(8,128)(2,1)S(1)}, bf16[128,256]{1,0:T(8,128)(2,1)S(1)}, u32[]{:S(2)}, u32[]{:S(2)}) %collective-permute-start.6) | collective-permute-done | bytes 65568 | tf_op jit(solution)/shard_map/grads_back/ppermute | solution.py:396
  74.6 0.0 collective-permute-done.5.refs_0_
  74.6 0.7 input_grad.1
  75.3 17.2 %all_to_all.21 = bf16[32,8,640]{2,1,0:T(8,128)(2,1)S(1)} all-to-all(bf16[32,8,640]{2,1,0:T(8,128)(2,1)S(1)} %bitcast.8), channel_id=1, replica_groups=mesh['x_hi'=2,'z'=8,'core'=2,'x_lo'=2,'y'=4] {'x_lo','x_hi','z'}, dimensions={0} | all-to-all | bytes 655360 | tf_op jit(solution)/shard_map/input_grad/all_to_all | solution.py:433
  92.6 0.7 reduce
Async XLA Ops:
  0.6 26.1 %copy-start.4 = (s32[64]{0:T(128)S(1)}, s32[64]{0:T(128)}, u32[]{:S(2)}) copy-start(s32[64]{0:T(128)} %param.22) | copy-start | bytes 772
  0.6 26.1 %copy-start.5 = (s32[16]{0:T(128)S(1)}, s32[16]{0:T(128)}, u32[]{:S(2)}) copy-start(s32[16]{0:T(128)} %param.23) | copy-start | bytes 196
  4.5 39.3 %copy-start.6 = (bf16[256,1024]{1,0:T(8,128)(2,1)S(1)}, bf16[256,1024]{1,0:T(8,128)(2,1)}, u32[]{:S(2)}) copy-start(bf16[256,1024]{1,0:T(8,128)(2,1)} %q_ref.1) | copy-start | bytes 1572868
  4.5 39.3 %copy-start.7 = (bf16[256,1024]{1,0:T(8,128)(2,1)S(1)}, bf16[256,1024]{1,0:T(8,128)(2,1)}, u32[]{:S(2)}) copy-start(bf16[256,1024]{1,0:T(8,128)(2,1)} %g_ref.1) | copy-start | bytes 1572868
  4.5 39.3 %copy-start.8 = (bf16[256,128]{1,0:T(8,128)(2,1)S(1)}, bf16[256,128]{1,0:T(8,128)(2,1)}, u32[]{:S(2)}) copy-start(bf16[256,128]{1,0:T(8,128)(2,1)} %rk_ref.1) | copy-start | bytes 196612
  4.5 39.3 %copy-start.9 = (bf16[256,128]{1,0:T(8,128)(2,1)S(1)}, bf16[256,128]{1,0:T(8,128)(2,1)}, u32[]{:S(2)}) copy-start(bf16[256,128]{1,0:T(8,128)(2,1)} %rv_ref.1) | copy-start | bytes 196612
  4.5 39.3 %copy-start.10 = (s32[32]{0:T(128)S(1)}, s32[32]{0:T(128)}, u32[]{:S(2)}) copy-start(s32[32]{0:T(128)} %param.21) | copy-start | bytes 388
  4.6 39.3 %copy-start.11 = (s32[16]{0:T(128)S(1)}, s32[16]{0:T(128)}, u32[]{:S(2)}) copy-start(s32[16]{0:T(128)} %param.24) | copy-start | bytes 196
  4.6 20.8 %all-to-all-start = ((bf16[16,32,128]{2,1,0:T(8,128)(2,1)}), bf16[16,32,128]{2,1,0:T(8,128)(2,1)S(1)}, u32[]{:S(2)}, u32[]{:S(2)}) async-start(bf16[16,32,128]{2,1,0:T(8,128)(2,1)} %get-tuple-element.19), calls=%async_computation | async-start | bytes 262144 | tf_op jit(solution)/shard_map/keys_out/all_to_all | solution.py:400
  15.8 19.0 %collective-permute-start.1 = (bf16[2,2,640,128]{3,2,1,0:T(8,128)(2,1)}, bf16[2,2,640,128]{3,2,1,0:T(8,128)(2,1)S(1)}, u32[]{:S(2)}, u32[]{:S(2)}) collective-permute-start(bf16[2,2,640,128]{3,2,1,0:T(8,128)(2,1)} %get-tuple-element.20), channel_id=1, source_target_pairs={{0,1},{1,0},{2,3},{3,2},{4,5},{5,4},{6,7},{7,6},{8,9},{9,8},{10,11... | collective-permute-start | bytes 1966088 | tf_op jit(solution)/shard_map/keys_out/ppermute | solution.py:396
  17.3 17.5 %collective-permute-start.2 = (bf16[2,2,640,128]{3,2,1,0:T(8,128)(2,1)}, bf16[2,2,640,128]{3,2,1,0:T(8,128)(2,1)S(1)}, u32[]{:S(2)}, u32[]{:S(2)}) collective-permute-start(bf16[2,2,640,128]{3,2,1,0:T(8,128)(2,1)} %get-tuple-element.21), channel_id=1, source_target_pairs={{0,3},{1,2},{2,1},{3,0},{4,7},{5,6},{6,5},{7,4},{8,11},{9,10},{10,... | collective-permute-start | bytes 1966088 | tf_op jit(solution)/shard_map/keys_out/ppermute | solution.py:396
  25.4 1.3 %collective-permute-start = (bf16[16,32,128]{2,1,0:T(8,128)(2,1)S(1)}, bf16[16,32,128]{2,1,0:T(8,128)(2,1)S(1)}, u32[]{:S(2)}, u32[]{:S(2)}) collective-permute-start(bf16[16,32,128]{2,1,0:T(8,128)(2,1)S(1)} %all-to-all-done.mine_ref.units_ref), channel_id=1, source_target_pairs={{0,8},{8,0},{1,9},{9,1},{2,10},{10,2},{3,11},{11,3},{4,12},{12,4},... | collective-permute-start | bytes 393224 | tf_op jit(solution)/shard_map/keys_out/ppermute | solution.py:404
  27.7 16.1 %all-to-all-start.1 = ((bf16[16,2,2,16,128]{4,3,2,1,0:T(8,128)(2,1)}), bf16[16,2,2,16,128]{4,3,2,1,0:T(8,128)(2,1)S(1)}, u32[]{:S(2)}, u32[]{:S(2)}) async-start(bf16[16,2,2,16,128]{4,3,2,1,0:T(8,128)(2,1)} %select.1), calls=%async_computation.1 | async-start | bytes 524288 | tf_op jit(solution)/shard_map/keys_out/all_to_all | solution.py:400
  31.6 32.8 %collective-permute-start.3 = (bf16[2,2,640,128]{3,2,1,0:T(8,128)(2,1)}, bf16[2,2,640,128]{3,2,1,0:T(8,128)(2,1)S(1)}, u32[]{:S(2)}, u32[]{:S(2)}) collective-permute-start(bf16[2,2,640,128]{3,2,1,0:T(8,128)(2,1)} %get-tuple-element.29), channel_id=1, source_target_pairs={{0,2},{1,3},{2,0},{3,1},{4,6},{5,7},{6,4},{7,5},{8,10},{9,11},{10,... | collective-permute-start | bytes 1966088 | tf_op jit(solution)/shard_map/keys_out/ppermute | solution.py:396
  43.9 21.9 %copy-start.2 = (f32[2,128,128]{2,1,0:T(8,128)S(1)}, f32[2,128,128]{2,1,0:T(8,128)}, u32[]{:S(2)}) copy-start(f32[2,128,128]{2,1,0:T(8,128)} %constant.4.clone.table_ref) | copy-start | bytes 393220
  43.9 21.9 %copy-start.3 = (f32[128]{0:T(128)S(1)}, f32[128]{0:T(128)}, u32[]{:S(2)}) copy-start(f32[128]{0:T(128)} %param.16) | copy-start | bytes 1540
  43.9 26.3 %copy-start.1 = (bf16[5120,128]{1,0:T(8,128)(2,1)S(1)}, bf16[5120,128]{1,0:T(8,128)(2,1)}, u32[]{:S(2)}) copy-start(bf16[5120,128]{1,0:T(8,128)(2,1)} %wv_ref.3) | copy-start | bytes 3932164
  47.9 22.3 %copy-start = (bf16[5120,128]{1,0:T(8,128)(2,1)S(1)}, bf16[5120,128]{1,0:T(8,128)(2,1)}, u32[]{:S(2)}) copy-start(bf16[5120,128]{1,0:T(8,128)(2,1)} %wk_ref.3) | copy-start | bytes 3932164
  64.4 1.3 %collective-permute-start.4 = (bf16[16,16,128]{2,1,0:T(8,128)(2,1)S(1)}, bf16[16,16,128]{2,1,0:T(8,128)(2,1)S(1)}, u32[]{:S(2)}, u32[]{:S(2)}) collective-permute-start(bf16[16,16,128]{2,1,0:T(8,128)(2,1)S(1)} %get-tuple-element.30), channel_id=1, source_target_pairs={{0,8},{8,0},{1,9},{9,1},{2,10},{10,2},{3,11},{11,3},{4,12},{12,4},... | collective-permute-start | bytes 196616 | tf_op jit(solution)/shard_map/grads_back/ppermute | solution.py:404
  66.0 5.9 %collective-permute-start.7 = (bf16[128,256]{1,0:T(8,128)(2,1)S(1)}, bf16[128,256]{1,0:T(8,128)(2,1)S(1)}, u32[]{:S(2)}, u32[]{:S(2)}) collective-permute-start(bf16[128,256]{1,0:T(8,128)(2,1)S(1)} %unkey.1.grads_ref), channel_id=1, source_target_pairs={{0,2},{1,3},{2,0},{3,1},{4,6},{5,7},{6,4},{7,5},{8,10},{9,11},{10,... | collective-permute-start | bytes 196616 | tf_op jit(solution)/shard_map/grads_back/ppermute | solution.py:396
  69.1 5.5 %collective-permute-start.6 = (bf16[128,256]{1,0:T(8,128)(2,1)S(1)}, bf16[128,256]{1,0:T(8,128)(2,1)S(1)}, u32[]{:S(2)}, u32[]{:S(2)}) collective-permute-start(bf16[128,256]{1,0:T(8,128)(2,1)S(1)} %unkey.1.grads_ref), channel_id=1, source_target_pairs={{0,3},{1,2},{2,1},{3,0},{4,7},{5,6},{6,5},{7,4},{8,11},{9,10},{10,... | collective-permute-start | bytes 196616 | tf_op jit(solution)/shard_map/grads_back/ppermute | solution.py:396
  70.2 4.4 %collective-permute-start.5 = (bf16[128,256]{1,0:T(8,128)(2,1)S(1)}, bf16[128,256]{1,0:T(8,128)(2,1)S(1)}, u32[]{:S(2)}, u32[]{:S(2)}) collective-permute-start(bf16[128,256]{1,0:T(8,128)(2,1)S(1)} %unkey.1.grads_ref), channel_id=1, source_target_pairs={{0,1},{1,0},{2,3},{3,2},{4,5},{5,4},{6,7},{7,6},{8,9},{9,8},{10,11... | collective-permute-start | bytes 196616 | tf_op jit(solution)/shard_map/grads_back/ppermute | solution.py:396
